TPU v7x, 32 devices: a whole 2x2x4 slice. The times are simulated.
32 devices in a mesh: dp: 4 (over y, core), seq: 8 (over z, x).
Axes of the slice: x: 2, y: 2, z: 4, core: 2. Of those that a mesh axis runs over, the one named last changes fastest.
Arguments:
- hidden_in: bfloat16 [8, 1024, 1408], P('dp', 'seq'), may hold values from -6 to 6
- skip_in: bfloat16 [8, 1024, 1408], P('dp', 'seq'), may hold values from -6 to 6
- text_states: bfloat16 [8, 333, 1024], P('dp', None, 'seq'), may hold values from -6 to 6
- timesteps: int32 [8], P('dp'), may hold values from 0 to 999
- positions: int32 [8, 2, 1024], P('dp', None, 'seq'), may hold values from 0 to 63, as said below
- cotangent: bfloat16 [8, 1024, 1408], P('dp', 'seq'), may hold values from -6 to 6
- skip_gain: float32 [2816], replicated, may hold values from 0.1 to 1.9
- skip_weight: bfloat16 [2816, 1408], P('dp'), may hold values from -0.109375 to 0.109375
- self_norm_gain: float32 [1408], replicated, may hold values from 0.1 to 1.9
- shift_weight: bfloat16 [1408, 1408], P('dp'), may hold values from -0.21875 to 0.21875
- qkv_weight: bfloat16 [1408, 4224], P('dp'), may hold values from -0.15625 to 0.15625
- query_gain: float32 [88], replicated, may hold values from 0.1 to 1.9
- key_gain: float32 [88], replicated, may hold values from 0.1 to 1.9
- self_out_weight: bfloat16 [1408, 1408], P('dp'), may hold values from -6 to 6
- cross_norm_gain: float32 [1408], replicated, may hold values from 0.1 to 1.9
- cross_query_weight: bfloat16 [1408, 1408], P('dp'), may hold values from -0.15625 to 0.15625
- text_kv_weight: bfloat16 [1024, 16, 176], P('dp', 'seq'), may hold values from -0.1875 to 0.1875
- cross_query_gain: float32 [88], replicated, may hold values from 0.1 to 1.9
- cross_key_gain: float32 [88], replicated, may hold values from 0.1 to 1.9
- cross_out_weight: bfloat16 [1408, 1408], P('dp'), may hold values from -3 to 3
- ffn_norm_gain: float32 [1408], replicated, may hold values from 0.1 to 1.9
- ffn_up_weight: bfloat16 [1408, 6144], P('dp'), may hold values from -0.15625 to 0.15625
- ffn_down_weight: bfloat16 [6144, 1408], P('dp'), may hold values from -0.078125 to 0.078125
Outputs:
- block_out: bfloat16 [8, 1024, 1408], P('dp', 'seq')
- hidden_grad: bfloat16 [8, 1024, 1408], P('dp', 'seq')
- skip_grad: bfloat16 [8, 1024, 1408], P('dp', 'seq')
- text_grad: bfloat16 [8, 333, 1024], P('dp', None, 'seq')
- skip_gain_grad: float32 [2816], replicated
- skip_weight_grad: float32 [2816, 1408], P('dp')
- self_norm_gain_grad: float32 [1408], replicated
- shift_weight_grad: float32 [1408, 1408], P('dp')
- qkv_weight_grad: float32 [1408, 4224], P('dp')
- query_gain_grad: float32 [88], replicated
- key_gain_grad: float32 [88], replicated
- self_out_weight_grad: float32 [1408, 1408], P('dp')
- cross_norm_gain_grad: float32 [1408], replicated
- cross_query_weight_grad: float32 [1408, 1408], P('dp')
- text_kv_weight_grad: float32 [1024, 16, 176], P('dp', 'seq')
- cross_query_gain_grad: float32 [88], replicated
- cross_key_gain_grad: float32 [88], replicated
- cross_out_weight_grad: float32 [1408, 1408], P('dp')
- ffn_norm_gain_grad: float32 [1408], replicated
- ffn_up_weight_grad: float32 [1408, 6144], P('dp')
- ffn_down_weight_grad: float32 [6144, 1408], P('dp')
Inputs may be any that keep to these rules, and one draw needn't show every extreme that they name: `positions`: each latent's tokens lie in row-major order on a grid of 16, 32 or 64 columns; entry 0 is a token's grid row, entry 1 its column.
All inputs are finite; a program needn't handle non-finite values.
Results may differ from a plain program's by a relative error of at most 0.023.
Values may be sent and summed in bfloat16 or wider, within the bound.
No kernel may reach another device: no remote copies, remote signals or barrier semaphores. Data moves between devices by JAX's collectives and lax.ppermute only.
A program may use at most 320 MiB of HBM per device.

v0:
```python
from functools import partial
import math

import jax
import jax.numpy as jnp
from jax import lax
from jax.sharding import PartitionSpec as P

H = 16
HD = 88


norm_eps = 1e-06


def layer_norm(tensor, gain_vec):
    center = tensor - jnp.mean(tensor, axis=-1, keepdims=True)
    spread = jnp.mean(center * center, axis=-1, keepdims=True)
    return center * lax.rsqrt(spread + norm_eps) * gain_vec


def matmul(left_side, right_side):
    return jnp.dot(left_side, right_side, preferred_element_type=jnp.float32)


def matmul_tn(left_side, right_side):
    return lax.dot_general(
        left_side, right_side, (((0,), (0,)), ((), ())), preferred_element_type=jnp.float32
    )


def matmul_nt(left_side, right_side):
    return lax.dot_general(
        left_side, right_side, (((1,), (1,)), ((), ())), preferred_element_type=jnp.float32
    )


def time_embed(step_ids, embed_width):
    half_width = embed_width // 2
    frequency = jnp.exp(-math.log(10000.0) * jnp.arange(half_width, dtype=jnp.float32) / half_width)
    angles = step_ids.astype(jnp.float32)[:, None] * frequency[None, :]
    return jnp.concatenate([jnp.cos(angles), jnp.sin(angles)], axis=-1)


def rope_tables(grid_pos, head_dim):
    quarter = head_dim // 4
    frequency = jnp.exp(-math.log(10000.0) * jnp.arange(quarter, dtype=jnp.float32) / quarter)
    row_angle = grid_pos[:, 0, :].astype(jnp.float32)[:, :, None, None] * frequency
    col_angle = grid_pos[:, 1, :].astype(jnp.float32)[:, :, None, None] * frequency
    return (jnp.cos(row_angle), jnp.sin(row_angle), jnp.cos(col_angle), jnp.sin(col_angle))


def rotate(tensor, tables):
    cos_row, sin_row, cos_col, sin_col = tables
    quarter = tensor.shape[-1] // 4
    first_part = tensor[..., :quarter]
    second_part = tensor[..., quarter : 2 * quarter]
    third_part = tensor[..., 2 * quarter : 3 * quarter]
    fourth_part = tensor[..., 3 * quarter :]
    return jnp.concatenate(
        [
            first_part * cos_row - second_part * sin_row,
            second_part * cos_row + first_part * sin_row,
            third_part * cos_col - fourth_part * sin_col,
            fourth_part * cos_col + third_part * sin_col,
        ],
        axis=-1,
    )


def to_heads(token_side):
    return lax.all_to_all(token_side, "seq", split_axis=3, concat_axis=1, tiled=True)


def to_tokens(head_side):
    return lax.all_to_all(head_side, "seq", split_axis=1, concat_axis=3, tiled=True)


def head_major(tensor, head_dim):
    batch_size, row_count, stack_count, width_part = tensor.shape
    shaped = tensor.reshape(batch_size, row_count, stack_count, width_part // head_dim, head_dim)
    return shaped.transpose(2, 0, 3, 1, 4)


def token_major(tensor):
    stack_count, batch_size, head_count, row_count, head_dim = tensor.shape
    return tensor.transpose(1, 3, 0, 2, 4).reshape(
        batch_size, row_count, stack_count, head_count * head_dim
    )


def split_rows(tensor, row_block):
    shaped = tensor.reshape(
        tensor.shape[:2] + (tensor.shape[2] // row_block, row_block) + tensor.shape[3:]
    )
    return jnp.moveaxis(shaped, 2, 0)


def join_rows(tensor):
    joined = jnp.moveaxis(tensor, 0, 2)
    return joined.reshape(
        joined.shape[:2] + (joined.shape[2] * joined.shape[3],) + joined.shape[4:]
    )


def attend_forward(queries, keys_in, values_in):
    row_block = min(512, queries.shape[2])
    score_scale = queries.shape[-1] ** (-0.5)

    def one_block(query_part):
        scores = score_scale * jnp.einsum(
            "bhqe,bhke->bhqk", query_part, keys_in, preferred_element_type=jnp.float32
        )
        row_max = jnp.max(scores, axis=-1, keepdims=True)
        exponent = jnp.exp(scores - row_max)
        row_total = jnp.sum(exponent, axis=-1, keepdims=True)
        weights_bf = (exponent / row_total).astype(jnp.bfloat16)
        output = jnp.einsum(
            "bhqk,bhke->bhqe", weights_bf, values_in, preferred_element_type=jnp.float32
        )
        return (output.astype(jnp.bfloat16), (row_max + jnp.log(row_total))[..., 0])

    outputs, log_sums = lax.map(one_block, split_rows(queries, row_block))
    return (join_rows(outputs), join_rows(log_sums))


def attend_backward(queries, keys_in, values_in, log_sums, grad_out):
    row_block = min(512, queries.shape[2])
    score_scale = queries.shape[-1] ** (-0.5)

    def one_block(carry, pieces):
        key_acc, value_acc = carry
        query_part, grad_part, sum_part = pieces
        scores = score_scale * jnp.einsum(
            "bhqe,bhke->bhqk", query_part, keys_in, preferred_element_type=jnp.float32
        )
        probs_full = jnp.exp(scores - sum_part[..., None])
        grad_probs = jnp.einsum(
            "bhqe,bhke->bhqk", grad_part, values_in, preferred_element_type=jnp.float32
        )
        row_dot = jnp.sum(grad_probs * probs_full, axis=-1, keepdims=True)
        grad_scores = (probs_full * (grad_probs - row_dot)).astype(jnp.bfloat16)
        grad_query = score_scale * jnp.einsum(
            "bhqk,bhke->bhqe", grad_scores, keys_in, preferred_element_type=jnp.float32
        )
        key_acc = key_acc + jnp.einsum(
            "bhqk,bhqe->bhke", grad_scores, query_part, preferred_element_type=jnp.float32
        )
        value_acc = value_acc + jnp.einsum(
            "bhqk,bhqe->bhke",
            probs_full.astype(jnp.bfloat16),
            grad_part,
            preferred_element_type=jnp.float32,
        )
        return ((key_acc, value_acc), grad_query)

    start_acc = (jnp.zeros(keys_in.shape, jnp.float32), jnp.zeros(values_in.shape, jnp.float32))
    (key_acc, value_acc), grad_queries = lax.scan(
        one_block,
        start_acc,
        (
            split_rows(queries, row_block),
            split_rows(grad_out, row_block),
            split_rows(log_sums, row_block),
        ),
    )
    return (join_rows(grad_queries), score_scale * key_acc, value_acc)


def local(
    hidden_in,
    skip_in,
    text_states,
    timesteps,
    positions,
    cotangent,
    skip_gain,
    skip_weight,
    self_norm_gain,
    shift_weight,
    qkv_weight,
    query_gain,
    key_gain,
    self_out_weight,
    cross_norm_gain,
    cross_query_weight,
    text_kv_weight,
    cross_query_gain,
    cross_key_gain,
    cross_out_weight,
    ffn_norm_gain,
    ffn_up_weight,
    ffn_down_weight,
):
    (
        skip_full,
        shift_full,
        qkv_full,
        self_out_full,
        cross_query_full,
        text_kv_full,
        cross_out_full,
        ffn_up_full,
        ffn_down_full,
    ) = (
        lax.all_gather(skip_weight, "dp", axis=0, tiled=True),
        lax.all_gather(shift_weight, "dp", axis=0, tiled=True),
        lax.all_gather(qkv_weight, "dp", axis=0, tiled=True),
        lax.all_gather(self_out_weight, "dp", axis=0, tiled=True),
        lax.all_gather(cross_query_weight, "dp", axis=0, tiled=True),
        lax.all_gather(text_kv_weight, "dp", axis=0, tiled=True),
        lax.all_gather(cross_out_weight, "dp", axis=0, tiled=True),
        lax.all_gather(ffn_up_weight, "dp", axis=0, tiled=True),
        lax.all_gather(ffn_down_weight, "dp", axis=0, tiled=True),
    )
    text_full = lax.all_gather(text_states, "seq", axis=2, tiled=True)
    batch_size, local_len, model_width = hidden_in.shape
    token_rows = batch_size * local_len
    tables = rope_tables(positions, HD)
    shift_embed = jax.nn.silu(time_embed(timesteps, model_width)).astype(jnp.bfloat16)
    joined = jnp.concatenate([hidden_in.astype(jnp.float32), skip_in.astype(jnp.float32)], axis=-1)
    normed_skip, skip_pull = jax.vjp(layer_norm, joined, skip_gain)
    skip_bf = normed_skip.astype(jnp.bfloat16).reshape(token_rows, 2 * model_width)
    stream_one = matmul(skip_bf, skip_full).reshape(batch_size, local_len, model_width)
    shift_vec = matmul(shift_embed, shift_full)
    normed_one, one_pull = jax.vjp(layer_norm, stream_one, self_norm_gain)
    first_bf = (
        (normed_one + shift_vec[:, None, :]).astype(jnp.bfloat16).reshape(token_rows, model_width)
    )
    qkv_raw = matmul(first_bf, qkv_full).reshape(batch_size, local_len, 3, H, HD)

    def head_piece(raw_heads, gain_vec):
        return rotate(layer_norm(raw_heads, gain_vec), tables)

    query_rot, query_pull = jax.vjp(head_piece, qkv_raw[:, :, 0], query_gain)
    key_rot, key_pull = jax.vjp(head_piece, qkv_raw[:, :, 1], key_gain)
    stacked = jnp.stack(
        [
            query_rot.astype(jnp.bfloat16),
            key_rot.astype(jnp.bfloat16),
            qkv_raw[:, :, 2].astype(jnp.bfloat16),
        ],
        axis=2,
    ).reshape(batch_size, local_len, 3, model_width)
    self_heads = head_major(to_heads(stacked), HD)
    self_out, self_sums = attend_forward(self_heads[0], self_heads[1], self_heads[2])
    self_tokens = to_tokens(token_major(self_out[None])).reshape(token_rows, model_width)
    stream_two = stream_one + matmul(self_tokens, self_out_full).reshape(
        batch_size, local_len, model_width
    )
    normed_two, two_pull = jax.vjp(layer_norm, stream_two, cross_norm_gain)
    second_bf = normed_two.astype(jnp.bfloat16).reshape(token_rows, model_width)
    cross_raw = matmul(second_bf, cross_query_full).reshape(batch_size, local_len, H, HD)
    cross_normed, cross_pull = jax.vjp(layer_norm, cross_raw, cross_query_gain)
    cross_heads = head_major(
        to_heads(cross_normed.astype(jnp.bfloat16).reshape(batch_size, local_len, 1, model_width)),
        HD,
    )[0]
    text_kv = jnp.einsum(
        "bmc,che->bhme", text_full, text_kv_full, preferred_element_type=jnp.float32
    )
    text_keys_full, text_key_pull = jax.vjp(layer_norm, text_kv[..., :HD], cross_key_gain)
    text_keys = text_keys_full.astype(jnp.bfloat16)
    text_values = text_kv[..., HD:].astype(jnp.bfloat16)
    cross_out, cross_sums = attend_forward(cross_heads, text_keys, text_values)
    cross_tokens = to_tokens(token_major(cross_out[None])).reshape(token_rows, model_width)
    stream_three = stream_two + matmul(cross_tokens, cross_out_full).reshape(
        batch_size, local_len, model_width
    )
    normed_three, three_pull = jax.vjp(layer_norm, stream_three, ffn_norm_gain)
    third_bf = normed_three.astype(jnp.bfloat16).reshape(token_rows, model_width)
    ffn_hidden = matmul(third_bf, ffn_up_full)
    activated, gelu_pull = jax.vjp(partial(jax.nn.gelu, approximate=True), ffn_hidden)
    activated_bf = activated.astype(jnp.bfloat16)
    block_out = stream_three + matmul(activated_bf, ffn_down_full).reshape(
        batch_size, local_len, model_width
    )
    grad_four = cotangent.reshape(token_rows, model_width)
    grad_active = matmul_nt(grad_four, ffn_down_full)
    grad_hidden = gelu_pull(grad_active)[0].astype(jnp.bfloat16)
    grad_three_norm = matmul_nt(grad_hidden, ffn_up_full).reshape(
        batch_size, local_len, model_width
    )
    back_three, ffn_gain_grad = three_pull(grad_three_norm)
    grad_three = cotangent.astype(jnp.float32) + back_three
    grad_three_bf = grad_three.astype(jnp.bfloat16).reshape(token_rows, model_width)
    grad_cross_tok = matmul_nt(grad_three_bf, cross_out_full).astype(jnp.bfloat16)
    grad_cross_heads = head_major(
        to_heads(grad_cross_tok.reshape(batch_size, local_len, 1, model_width)), HD
    )[0]
    grad_cq_heads, grad_text_keys, grad_text_values = attend_backward(
        cross_heads, text_keys, text_values, cross_sums, grad_cross_heads
    )
    grad_cq_tok = to_tokens(token_major(grad_cq_heads.astype(jnp.bfloat16)[None])).reshape(
        batch_size, local_len, H, HD
    )
    back_cross, cross_query_gain_grad = cross_pull(grad_cq_tok.astype(jnp.float32))
    grad_cross_raw = back_cross.astype(jnp.bfloat16).reshape(token_rows, model_width)
    grad_two_norm = matmul_nt(grad_cross_raw, cross_query_full).reshape(
        batch_size, local_len, model_width
    )
    back_two, cross_norm_grad = two_pull(grad_two_norm)
    grad_two = grad_three + back_two
    back_keys, cross_key_gain_grad = text_key_pull(grad_text_keys)
    grad_text_kv = jnp.concatenate([back_keys, grad_text_values], axis=-1).astype(jnp.bfloat16)
    text_kv_grad = jnp.einsum(
        "bmc,bhme->che", text_full, grad_text_kv, preferred_element_type=jnp.float32
    )
    text_part = jnp.einsum(
        "bhme,che->bmc", grad_text_kv, text_kv_full, preferred_element_type=jnp.float32
    )
    text_grad = lax.psum_scatter(
        text_part.astype(jnp.bfloat16), "seq", scatter_dimension=2, tiled=True
    )
    grad_two_bf = grad_two.astype(jnp.bfloat16).reshape(token_rows, model_width)
    grad_self_tok = matmul_nt(grad_two_bf, self_out_full).astype(jnp.bfloat16)
    grad_self_heads = head_major(
        to_heads(grad_self_tok.reshape(batch_size, local_len, 1, model_width)), HD
    )[0]
    grad_query, grad_key, grad_value = attend_backward(
        self_heads[0], self_heads[1], self_heads[2], self_sums, grad_self_heads
    )
    grad_stack = jnp.stack([grad_query, grad_key, grad_value]).astype(jnp.bfloat16)
    grad_qkv_tok = to_tokens(token_major(grad_stack))
    back_query, query_gain_grad = query_pull(
        grad_qkv_tok[:, :, 0].reshape(batch_size, local_len, H, HD).astype(jnp.float32)
    )
    back_key, key_gain_grad = key_pull(
        grad_qkv_tok[:, :, 1].reshape(batch_size, local_len, H, HD).astype(jnp.float32)
    )
    grad_qkv = (
        jnp.stack(
            [
                back_query,
                back_key,
                grad_qkv_tok[:, :, 2].reshape(batch_size, local_len, H, HD).astype(jnp.float32),
            ],
            axis=2,
        )
        .astype(jnp.bfloat16)
        .reshape(token_rows, 3 * model_width)
    )
    grad_one_norm = matmul_nt(grad_qkv, qkv_full).reshape(batch_size, local_len, model_width)
    shift_part = jnp.sum(grad_one_norm, axis=1)
    back_one, self_norm_grad = one_pull(grad_one_norm)
    grad_one_bf = (grad_two + back_one).astype(jnp.bfloat16).reshape(token_rows, model_width)
    grad_skip_norm = matmul_nt(grad_one_bf, skip_full).reshape(
        batch_size, local_len, 2 * model_width
    )
    back_joined, skip_gain_grad = skip_pull(grad_skip_norm)
    hidden_grad = back_joined[..., :model_width].astype(jnp.bfloat16)
    skip_grad = back_joined[..., model_width:].astype(jnp.bfloat16)
    down_grad = matmul_tn(activated_bf, grad_four)
    up_grad = matmul_tn(third_bf, grad_hidden)
    cross_out_grad = matmul_tn(cross_tokens, grad_three_bf)
    cross_query_grad = matmul_tn(second_bf, grad_cross_raw)
    self_out_grad = matmul_tn(self_tokens, grad_two_bf)
    qkv_grad = matmul_tn(first_bf, grad_qkv)
    shift_grad = lax.dot_general(
        shift_embed.astype(jnp.float32),
        shift_part,
        (((0,), (0,)), ((), ())),
        precision=lax.Precision.HIGHEST,
        preferred_element_type=jnp.float32,
    )
    skip_weight_grad = matmul_tn(skip_bf, grad_one_bf)
    (
        skip_sum,
        shift_sum,
        qkv_sum,
        self_out_sum,
        cross_query_sum,
        cross_out_sum,
        up_sum,
        down_sum,
        text_kv_sum,
    ) = (
        lax.psum_scatter(
            skip_weight_grad.astype(jnp.bfloat16), "dp", scatter_dimension=0, tiled=True
        ).astype(jnp.float32),
        lax.psum_scatter(
            shift_grad.astype(jnp.bfloat16), "dp", scatter_dimension=0, tiled=True
        ).astype(jnp.float32),
        lax.psum_scatter(
            qkv_grad.astype(jnp.bfloat16), "dp", scatter_dimension=0, tiled=True
        ).astype(jnp.float32),
        lax.psum_scatter(
            self_out_grad.astype(jnp.bfloat16), "dp", scatter_dimension=0, tiled=True
        ).astype(jnp.float32),
        lax.psum_scatter(
            cross_query_grad.astype(jnp.bfloat16), "dp", scatter_dimension=0, tiled=True
        ).astype(jnp.float32),
        lax.psum_scatter(
            cross_out_grad.astype(jnp.bfloat16), "dp", scatter_dimension=0, tiled=True
        ).astype(jnp.float32),
        lax.psum_scatter(
            up_grad.astype(jnp.bfloat16), "dp", scatter_dimension=0, tiled=True
        ).astype(jnp.float32),
        lax.psum_scatter(
            down_grad.astype(jnp.bfloat16), "dp", scatter_dimension=0, tiled=True
        ).astype(jnp.float32),
        lax.psum_scatter(
            text_kv_grad.astype(jnp.bfloat16), "dp", scatter_dimension=0, tiled=True
        ).astype(jnp.float32),
    )
    skip_sum, shift_sum, qkv_sum, self_out_sum, cross_query_sum, cross_out_sum, up_sum, down_sum = (
        lax.psum(skip_sum.astype(jnp.bfloat16), "seq").astype(jnp.float32),
        lax.psum(shift_sum.astype(jnp.bfloat16), "seq").astype(jnp.float32),
        lax.psum(qkv_sum.astype(jnp.bfloat16), "seq").astype(jnp.float32),
        lax.psum(self_out_sum.astype(jnp.bfloat16), "seq").astype(jnp.float32),
        lax.psum(cross_query_sum.astype(jnp.bfloat16), "seq").astype(jnp.float32),
        lax.psum(cross_out_sum.astype(jnp.bfloat16), "seq").astype(jnp.float32),
        lax.psum(up_sum.astype(jnp.bfloat16), "seq").astype(jnp.float32),
        lax.psum(down_sum.astype(jnp.bfloat16), "seq").astype(jnp.float32),
    )
    (
        skip_gain_sum,
        self_norm_sum,
        query_gain_sum,
        key_gain_sum,
        cross_norm_sum,
        cross_query_gain_sum,
        cross_key_gain_sum,
        ffn_gain_sum,
    ) = lax.psum(
        (
            skip_gain_grad,
            self_norm_grad,
            query_gain_grad,
            key_gain_grad,
            cross_norm_grad,
            cross_query_gain_grad,
            cross_key_gain_grad,
            ffn_gain_grad,
        ),
        ("dp", "seq"),
    )
    return (
        block_out.astype(jnp.bfloat16),
        hidden_grad,
        skip_grad,
        text_grad,
        skip_gain_sum,
        skip_sum,
        self_norm_sum,
        shift_sum,
        qkv_sum,
        query_gain_sum,
        key_gain_sum,
        self_out_sum,
        cross_norm_sum,
        cross_query_sum,
        text_kv_sum,
        cross_query_gain_sum,
        cross_key_gain_sum,
        cross_out_sum,
        ffn_gain_sum,
        up_sum,
        down_sum,
    )


def solution(mesh):
    placed = (
        P("dp", "seq", None),
        P("dp", "seq", None),
        P("dp", None, "seq"),
        P("dp"),
        P("dp", None, "seq"),
        P("dp", "seq", None),
        P(),
        P("dp", None),
        P(),
        P("dp", None),
        P("dp", None),
        P(),
        P(),
        P("dp", None),
        P(),
        P("dp", None),
        P("dp", "seq", None),
        P(),
        P(),
        P("dp", None),
        P(),
        P("dp", None),
        P("dp", None),
    )
    return jax.shard_map(
        local,
        mesh=mesh,
        in_specs=placed,
        out_specs=(
            P("dp", "seq", None),
            P("dp", "seq", None),
            P("dp", "seq", None),
            P("dp", None, "seq"),
            P(),
            P("dp", None),
            P(),
            P("dp", None),
            P("dp", None),
            P(),
            P(),
            P("dp", None),
            P(),
            P("dp", None),
            P("dp", "seq", None),
            P(),
            P(),
            P("dp", None),
            P(),
            P("dp", None),
            P("dp", None),
        ),
        check_vma=False,
    )
```

profile of v0, /device:TPU:1, one launch (start us, length us, event | category | flops | bytes accessed | tf_op | source)
XLA Modules:
  0.0 2041.8 jit_solution(16562237684557367779)
XLA Ops:
  17.2 28.1 %all-gather.12.cloned.1.call-done = bf16[1408,1408]{1,0:T(8,128)(2,1)} async-done(((bf16[352,1408]{1,0:T(8,128)(2,1)}), bf16[1408,1408]{1,0:T(8,128)(2,1)}) %all-gather.12.cloned.1.call-update) | async-done | bytes 3964944 | tf_op jit(solution)/shard_map/all_gather | solution.py:207
  48.1 54.5 %all-gather.10.cloned.1.call-done = bf16[2816,1408]{1,0:T(8,128)(2,1)} async-done(((bf16[704,1408]{1,0:T(8,128)(2,1)}), bf16[2816,1408]{1,0:T(8,128)(2,1)}) %all-gather.10.cloned.1.call-update) | async-done | bytes 7929872 | tf_op jit(solution)/shard_map/all_gather | solution.py:206
  109.9 72.5 %all-gather.14.cloned.1.call-done = bf16[1408,4224]{1,0:T(8,128)(2,1)} async-done(((bf16[352,4224]{1,0:T(8,128)(2,1)}), bf16[1408,4224]{1,0:T(8,128)(2,1)}) %all-gather.14.cloned.1.call-update) | async-done | bytes 11894800 | tf_op jit(solution)/shard_map/all_gather | solution.py:208
  182.4 16.9 copy.199
  238.0 54.9 %all-to-all-done = bf16[2,128,3,1408]{1,0,2,3:T(2,128)(2,1)} async-done(((bf16[2,128,3,1408]{1,0,2,3:T(2,128)(2,1)}), bf16[2,128,3,1408]{1,0,2,3:T(2,128)(2,1)}, u32[]{:S(2)}, u32[]{:S(2)}) %all-to-all-start) | async-done | bytes 2162720 | tf_op jit(solution)/shard_map/all_to_all | solution.py:72
  307.4 12.2 while.54
  333.9 13.3 all_gather.35
  383.5 13.9 all-to-all-done.2
  408.5 30.6 %all_to_all.118 = bf16[2,1024,1,176]{3,0,2,1:T(2,128)(2,1)S(1)} all-to-all(bf16[2,1024,1,176]{3,0,2,1:T(2,128)(2,1)} %copy.220), channel_id=1, replica_groups=mesh['dp'=4,'seq'=8] {'seq'}, dimensions={1} | all-to-all | bytes 1441792 | tf_op jit(solution)/shard_map/all_to_all | solution.py:76
  445.9 14.2 all-gather.26.cloned.1.call-done
  460.2 18.8 fusion.155
  478.9 94.2 %all-gather.24.cloned.1.call-done = bf16[1408,6144]{1,0:T(8,128)(2,1)} async-done(((bf16[352,6144]{1,0:T(8,128)(2,1)}), bf16[1408,6144]{1,0:T(8,128)(2,1)}) %all-gather.24.cloned.1.call-update) | async-done | bytes 17301520 | tf_op jit(solution)/shard_map/all_gather | solution.py:213
  573.1 15.7 fusion.76
  588.8 10.5 fusion.156
  600.5 13.1 fusion.144
  633.8 11.9 all-to-all-done.4
  648.7 20.0 while.56
  672.0 29.6 %all_to_all.117 = bf16[2,1024,1,176]{3,0,2,1:T(2,128)(2,1)S(1)} all-to-all(bf16[2,1024,1,176]{3,0,2,1:T(2,128)(2,1)S(1)} %copy.232), channel_id=1, replica_groups=mesh['dp'=4,'seq'=8] {'seq'}, dimensions={1} | all-to-all | bytes 1441792 | tf_op jit(solution)/shard_map/all_to_all | solution.py:76
  725.0 13.0 all-to-all-done.6
  744.2 38.9 %while.57 = (s32[]{:T(128)}, f32[2,2,1024,88]{2,3,1,0:T(8,128)}, f32[2,2,1024,88]{2,3,1,0:T(8,128)S(1)}, bf16[2,2,2,512,88]{3,4,2,1,0:T(8,128)(2,1)}, bf16[2,2,2...) while((s32[]{:T(128)}, f32[2,2,1024,88]{2,3,1,0:T(8,128)}, ...), condition=%wide.region_36.37_spmd.clone, body=%wide.region_34.36_spmd.clone.sunk | while | flops 1872279552 | bytes 148824880 | solution.py:158
  806.0 62.1 %all-to-all-done.7 = bf16[2,1024,3,176]{3,0,2,1:T(2,128)(2,1)S(1)} async-done(((bf16[2,1024,3,176]{3,0,2,1:T(2,128)(2,1)}), bf16[2,1024,3,176]{3,0,2,1:T(2,128)(2,1)S(1)}, u32[]{:S(2)}, u32[]{:S(2)}) %all-to-all-start.7) | async-done | bytes 2162720 | tf_op jit(solution)/shard_map/all_to_all | solution.py:76
  911.8 7.8 convolution_convert_fusion.2
  920.7 12.6 convolution_convert_fusion.1
  934.4 11.4 convolution_convert_fusion
  962.6 48.7 %reduce-scatter.13.cloned.1.call-done = bf16[704,1408]{1,0:T(8,128)(2,1)} async-done(((bf16[2816,1408]{1,0:T(8,128)(2,1)}), bf16[704,1408]{1,0:T(8,128)(2,1)}) %reduce-scatter.13.cloned.1.call-update) | async-done | bytes 1982480 | tf_op jit(solution)/shard_map/reduce_scatter | solution.py:378
  1011.3 97.0 %reduce-scatter.17.cloned.1.call-done = bf16[352,4224]{1,0:T(8,128)(2,1)} async-done(((bf16[1408,4224]{1,0:T(8,128)(2,1)}), bf16[352,4224]{1,0:T(8,128)(2,1)}) %reduce-scatter.17.cloned.1.call-update) | async-done | bytes 2973712 | tf_op jit(solution)/shard_map/reduce_scatter | solution.py:384
  1108.3 131.8 %reduce-scatter.27.cloned.1.call-done = bf16[352,6144]{1,0:T(8,128)(2,1)} async-done(((bf16[1408,6144]{1,0:T(8,128)(2,1)}), bf16[352,6144]{1,0:T(8,128)(2,1)}) %reduce-scatter.27.cloned.1.call-update) | async-done | bytes 4325392 | tf_op jit(solution)/shard_map/reduce_scatter | solution.py:396
  1240.1 131.9 %reduce-scatter.29.cloned.1.call-done = bf16[1536,1408]{1,0:T(8,128)(2,1)} async-done(((bf16[6144,1408]{1,0:T(8,128)(2,1)}), bf16[1536,1408]{1,0:T(8,128)(2,1)}) %reduce-scatter.29.cloned.1.call-update) | async-done | bytes 4325392 | tf_op jit(solution)/shard_map/reduce_scatter | solution.py:399
  1372.1 25.9 %reduce-scatter.23.cloned.1.call-done = bf16[256,2,176]{0,2,1:T(8,128)(2,1)} async-done(((bf16[1024,2,176]{0,2,1:T(8,128)(2,1)}), bf16[256,2,176]{0,2,1:T(8,128)(2,1)}) %reduce-scatter.23.cloned.1.call-update) | async-done | bytes 180240 | tf_op jit(solution)/shard_map/reduce_scatter | solution.py:402
  1399.6 66.5 %reduce-scatter.31.cloned.1.call-done = bf16[128,666]{1,0:T(8,128)(2,1)} async-done(((bf16[1024,666]{1,0:T(8,128)(2,1)}), bf16[128,666]{1,0:T(8,128)(2,1)}) %reduce-scatter.31.cloned.1.call-update) | async-done | bytes 170512
  1475.9 48.5 %all-reduce.8 = (f32[2816]{0:T(1024)}, f32[1408]{0:T(1024)}, f32[88]{0:T(128)}, f32[88]{0:T(128)}, f32[1408]{0:T(1024)}, /*index=5*/f32[88]{0:T(128)}, f32[88]{0:T(128)}, f32[1408]{0:T(1024)}) all-reduce(f32[2816]{0:T(1024)S(1)} %get-tuple-element.475, ...), channel_id=1, replica_groups=mesh['dp'=4,'seq'=8] {'dp','seq'}, use_global_device_ids=true, to_apply=%region_49.50 | all-reduce | flops 7392 | bytes 59136 | tf_op jit(solution)/shard_map/psum | solution.py:425
  1528.6 483.9 %all-reduce.12.cloned.1.call-done = (bf16[704,1408]{1,0:T(8,128)(2,1)}, bf16[352,1408]{1,0:T(8,128)(2,1)}, bf16[352,4224]{1,0:T(8,128)(2,1)}, bf16[352,1408]{1,0...) async-done(((bf16[704,1408]{1,0:T(8,128)(2,1)}, bf16[352,1408]{1,0:T(8,128)(2,1)}, ...) | async-done | bytes 17571856 | tf_op jit(solution)/shard_map/psum | solution.py:407
  (590 shorter events, 396.5 us)
Async XLA Ops:
  7.2 38.1 %all-gather.12.cloned.1.call-start = ((), (), s32[]{:S(2)}) async-start(), calls=%async_computation.19 | async-start | bytes 4956160 | tf_op jit(solution)/shard_map/all_gather | solution.py:207
  7.9 94.7 %all-gather.10.cloned.1.call-start = ((), (), s32[]{:S(2)}) async-start(), calls=%async_computation.18 | async-start | bytes 9912320 | tf_op jit(solution)/shard_map/all_gather | solution.py:206
  8.7 173.7 %all-gather.14.cloned.1.call-start = ((), (), s32[]{:S(2)}) async-start(), calls=%async_computation.20 | async-start | bytes 14868480 | tf_op jit(solution)/shard_map/all_gather | solution.py:208
  9.4 337.8 %all-gather.18.cloned.1.call-start = ((), (), s32[]{:S(2)}) async-start(), calls=%async_computation.22 | async-start | bytes 4956160 | tf_op jit(solution)/shard_map/all_gather | solution.py:210
  10.0 351.0 %all-gather.16.cloned.1.call-start = ((), (), s32[]{:S(2)}) async-start(), calls=%async_computation.21 | async-start | bytes 4956160 | tf_op jit(solution)/shard_map/all_gather | solution.py:209
  10.6 369.8 %all-gather.20.cloned.1.call-start = ((), (), s32[]{:S(2)}) async-start(), calls=%async_computation.23 | async-start | bytes 1548288 | tf_op jit(solution)/shard_map/all_gather | solution.py:216
  11.4 429.7 %all-gather.22.cloned.1.call-start = ((), (), s32[]{:S(2)}) async-start(), calls=%async_computation.24 | async-start | bytes 4956160 | tf_op jit(solution)/shard_map/all_gather | solution.py:212
  12.1 448.0 %all-gather.26.cloned.1.call-start = ((), (), s32[]{:S(2)}) async-start(), calls=%async_computation.26 | async-start | bytes 21626880 | tf_op jit(solution)/shard_map/all_gather | solution.py:214
  12.9 560.2 %all-gather.24.cloned.1.call-start = ((), (), s32[]{:S(2)}) async-start(), calls=%async_computation.25 | async-start | bytes 21626880 | tf_op jit(solution)/shard_map/all_gather | solution.py:213
  17.2 198.2 %copy-start.68 = (f32[2,128,22]{1,2,0:T(8,128)}, f32[2,128,22]{1,2,0:T(8,128)S(1)}, u32[]{:S(2)}) copy-start(f32[2,128,22]{1,2,0:T(8,128)S(1)} %get-tuple-element.625) | copy-start | bytes 67588
  17.2 198.2 %copy-start.70 = (f32[2,128,22]{1,2,0:T(8,128)}, f32[2,128,22]{1,2,0:T(8,128)S(1)}, u32[]{:S(2)}) copy-start(f32[2,128,22]{1,2,0:T(8,128)S(1)} %get-tuple-element.626) | copy-start | bytes 67588
  17.2 198.2 %copy-start.72 = (f32[2,128,22]{1,2,0:T(8,128)}, f32[2,128,22]{1,2,0:T(8,128)S(1)}, u32[]{:S(2)}) copy-start(f32[2,128,22]{1,2,0:T(8,128)S(1)} %get-tuple-element.629) | copy-start | bytes 67588
  17.2 198.2 %copy-start.74 = (f32[2,128,22]{1,2,0:T(8,128)}, f32[2,128,22]{1,2,0:T(8,128)S(1)}, u32[]{:S(2)}) copy-start(f32[2,128,22]{1,2,0:T(8,128)S(1)} %get-tuple-element.630) | copy-start | bytes 67588
  108.9 252.2 %copy-start.11 = (f32[2,128,1408]{2,1,0:T(8,128)}, f32[2,128,1408]{2,1,0:T(8,128)S(1)}, u32[]{:S(2)}) copy-start(f32[2,128,1408]{2,1,0:T(8,128)S(1)} %get-tuple-element.632) | copy-start | bytes 4325380
  232.7 60.1 %all-to-all-start = ((bf16[2,128,3,1408]{1,0,2,3:T(2,128)(2,1)}), bf16[2,128,3,1408]{1,0,2,3:T(2,128)(2,1)}, u32[]{:S(2)}, u32[]{:S(2)}) async-start(bf16[2,128,3,1408]{1,0,2,3:T(2,128)(2,1)} %pad_maximum_fusion), calls=%async_computation | async-start | bytes 4325376 | tf_op jit(solution)/shard_map/all_to_all | solution.py:72
  329.6 29.4 %all-to-all-start.1 = ((bf16[2,1024,1,176]{3,0,2,1:T(2,128)(2,1)}), bf16[2,1024,1,176]{3,0,2,1:T(2,128)(2,1)S(1)}, u32[]{:S(2)}, u32[]{:S(2)}) async-start(bf16[2,1024,1,176]{3,0,2,1:T(2,128)(2,1)} %copy.207), calls=%async_computation.1 | async-start | bytes 2097152 | tf_op jit(solution)/shard_map/all_to_all | solution.py:76
  375.9 21.5 %all-to-all-start.2 = ((bf16[2,128,1,1408]{1,0,2,3:T(2,128)(2,1)}), bf16[2,128,1,1408]{1,0,2,3:T(2,128)(2,1)S(1)}, u32[]{:S(2)}, u32[]{:S(2)}) async-start(bf16[2,128,1,1408]{1,0,2,3:T(2,128)(2,1)} %copy.212), calls=%async_computation.2 | async-start | bytes 1441792 | tf_op jit(solution)/shard_map/all_to_all | solution.py:72
  445.9 127.2 %copy-start.45 = (bf16[2,128,1408]{2,1,0:T(8,128)(2,1)}, bf16[2,128,1408]{2,1,0:T(8,128)(2,1)S(1)}, u32[]{:S(2)}) copy-start(bf16[2,128,1408]{2,1,0:T(8,128)(2,1)S(1)} %multiply_convert_fusion.5) | copy-start | bytes 2162692
  622.5 23.2 %all-to-all-start.4 = ((bf16[2,128,1,1408]{1,0,2,3:T(2,128)(2,1)}), bf16[2,128,1,1408]{1,0,2,3:T(2,128)(2,1)S(1)}, u32[]{:S(2)}, u32[]{:S(2)}) async-start(bf16[2,128,1,1408]{1,0,2,3:T(2,128)(2,1)} %copy.224), calls=%async_computation.4 | async-start | bytes 1441792 | tf_op jit(solution)/shard_map/all_to_all | solution.py:72
  627.7 334.8 %reduce-scatter.25.cloned.1.call-start = ((), (), s32[]{:S(2)}) async-start(), calls=%async_computation.33 | async-start | bytes 4956160 | tf_op jit(solution)/shard_map/reduce_scatter | solution.py:393
  716.6 21.4 %all-to-all-start.6 = ((bf16[2,128,1,1408]{1,0,2,3:T(2,128)(2,1)}), bf16[2,128,1,1408]{1,0,2,3:T(2,128)(2,1)}, u32[]{:S(2)}, u32[]{:S(2)}) async-start(bf16[2,128,1,1408]{1,0,2,3:T(2,128)(2,1)} %copy.236), calls=%async_computation.6 | async-start | bytes 1441792 | tf_op jit(solution)/shard_map/all_to_all | solution.py:72
  720.9 241.6 %reduce-scatter.21.cloned.1.call-start = ((), (), s32[]{:S(2)}) async-start(), calls=%async_computation.31 | async-start | bytes 4956160 | tf_op jit(solution)/shard_map/reduce_scatter | solution.py:390
  792.8 75.3 %all-to-all-start.7 = ((bf16[2,1024,3,176]{3,0,2,1:T(2,128)(2,1)}), bf16[2,1024,3,176]{3,0,2,1:T(2,128)(2,1)S(1)}, u32[]{:S(2)}, u32[]{:S(2)}) async-start(bf16[2,1024,3,176]{3,0,2,1:T(2,128)(2,1)} %copy.241), calls=%async_computation.7 | async-start | bytes 6291456 | tf_op jit(solution)/shard_map/all_to_all | solution.py:76
  798.2 164.3 %reduce-scatter.19.cloned.1.call-start = ((), (), s32[]{:S(2)}) async-start(), calls=%async_computation.30 | async-start | bytes 4956160 | tf_op jit(solution)/shard_map/reduce_scatter | solution.py:387
  806.0 156.6 %reduce-scatter.15.cloned.1.call-start = ((), (), s32[]{:S(2)}) async-start(), calls=%async_computation.28 | async-start | bytes 4956160 | tf_op jit(solution)/shard_map/reduce_scatter | solution.py:381
  896.5 114.8 %reduce-scatter.13.cloned.1.call-start = ((), (), s32[]{:S(2)}) async-start(), calls=%async_computation.27 | async-start | bytes 9912320 | tf_op jit(solution)/shard_map/reduce_scatter | solution.py:378
  907.7 200.6 %reduce-scatter.17.cloned.1.call-start = ((), (), s32[]{:S(2)}) async-start(), calls=%async_computation.29 | async-start | bytes 14868480 | tf_op jit(solution)/shard_map/reduce_scatter | solution.py:384
  919.6 320.5 %reduce-scatter.27.cloned.1.call-start = ((), (), s32[]{:S(2)}) async-start(), calls=%async_computation.34 | async-start | bytes 21626880 | tf_op jit(solution)/shard_map/reduce_scatter | solution.py:396
  933.3 438.7 %reduce-scatter.29.cloned.1.call-start = ((), (), s32[]{:S(2)}) async-start(), calls=%async_computation.35 | async-start | bytes 21626880 | tf_op jit(solution)/shard_map/reduce_scatter | solution.py:399
  945.9 452.1 %reduce-scatter.23.cloned.1.call-start = ((), (), s32[]{:S(2)}) async-start(), calls=%async_computation.32 | async-start | bytes 901120 | tf_op jit(solution)/shard_map/reduce_scatter | solution.py:402
  952.2 513.9 %reduce-scatter.31.cloned.1.call-start = ((), (), s32[]{:S(2)}) async-start(), calls=%async_computation.36 | async-start | bytes 1769472
  962.4 1050.1 %all-reduce.12.cloned.1.call-start = ((), (), s32[]{:S(2)}) async-start(), calls=%async_computation.37 | async-start | bytes 35143680 | tf_op jit(solution)/shard_map/psum | solution.py:407
  (142 other events, 1200.4 us)
Sparse Core Ops, SparseCore 0:
  9.6 35.6 all-gather.11
  46.9 55.6 all-gather.9
  104.2 78.1 all-gather.13
  183.8 33.1 all-gather.17
  218.4 33.1 all-gather.15
  254.1 52.8 all-gather.19
  308.6 38.7 all-gather.21
  349.0 111.1 all-gather.25
  461.7 111.3 all-gather.23
  633.9 43.3 reduce-scatter.24
  725.1 44.8 reduce-scatter.20
  806.1 44.0 reduce-scatter.18
  896.6 42.5 reduce-scatter.14
  942.2 68.9 reduce-scatter.12
  1013.8 94.5 reduce-scatter.16
  1110.8 129.2 reduce-scatter.26
  1242.7 129.2 reduce-scatter.28
  1375.0 22.8 reduce-scatter.22
  1402.3 63.7 reduce-scatter.30
  1471.6 540.8 all-reduce.11
where the time goes:
time: 2050 us; the launch traced here: 2040 us
  waiting for transfers between devices  1420 us (69%)
  matrix products  224 us (11%)
  local copies, waits for them, and re-layouts  164 us (8%)
  blocking collectives  122 us (6%)
  other arithmetic  68.1 us (3%)
  starting transfers between devices  30.4 us (1%)
    psum x1, waiting for transfers between devices, local(): lax.psum(skip_sum.astype(jnp.bfloat16), 'seq').astype(jnp.float32)  484 us
    reduce_scatter x1, waiting for transfers between devices, local(): lax.psum_scatter(down_grad.astype(jnp.bfloat16), 'dp', scatter_dimension=...  132 us
    reduce_scatter x1, waiting for transfers between devices, local(): lax.psum_scatter(up_grad.astype(jnp.bfloat16), 'dp', scatter_dimension=0,...  132 us
    reduce_scatter x1, waiting for transfers between devices, local(): lax.psum_scatter(qkv_grad.astype(jnp.bfloat16), 'dp', scatter_dimension=0...  97 us
    all_gather x1, waiting for transfers between devices, local(): lax.all_gather(ffn_up_weight, 'dp', axis=0, tiled=True)  94.2 us
    all_to_all x4, waiting for transfers between devices, to_heads(): lax.all_to_all(token_side, 'seq', split_axis=3, concat_axis=1, tiled=True)  93.6 us
    all_gather x1, waiting for transfers between devices, local(): lax.all_gather(qkv_weight, 'dp', axis=0, tiled=True)  72.5 us
    unnamed x21, waiting for transfers between devices  71.9 us
  transfers between devices with their start and end apart: 26, of which 18 were waited for; matrix products, arithmetic and copies ran while one was open for 18% of the time, Pallas kernels for 0%

commit v1 on v0

v1 whole, which is shorter than its diff:
```python
import math

import jax
import jax.numpy as jnp
from jax import lax
from jax.experimental import pallas as pl
from jax.experimental.pallas import tpu as pltpu
from jax.sharding import Mesh, PartitionSpec as P

H = 16
HD = 88
SCALE = HD ** (-0.5)
norm_eps = 1e-06
F32 = jnp.float32
BF = jnp.bfloat16
SEQ = ("z", "x")
SMALL = pl.CostEstimate(flops=1024, bytes_accessed=1024, transcendentals=0)


def dot(left, right, left_dim, right_dim):
    return lax.dot_general(
        left, right, (((left_dim,), (right_dim,)), ((), ())), preferred_element_type=F32
    )


def norm_stats(tensor, axis):
    mean = jnp.mean(tensor, axis=axis, keepdims=True)
    center = tensor - mean
    spread = jnp.mean(center * center, axis=axis, keepdims=True)
    return mean, lax.rsqrt(spread + norm_eps)


def norm_back(grad, tensor, mean, rstd, gain, axis):
    normed = (tensor - mean) * rstd
    scaled = grad * gain
    first = jnp.mean(scaled, axis=axis, keepdims=True)
    second = jnp.mean(scaled * normed, axis=axis, keepdims=True)
    return rstd * (scaled - first - normed * second), grad * normed


def time_embed(step_ids, embed_width):
    half_width = embed_width // 2
    frequency = jnp.exp(-math.log(10000.0) * jnp.arange(half_width, dtype=F32) / half_width)
    angles = step_ids.astype(F32)[:, None] * frequency[None, :]
    return jnp.concatenate([jnp.cos(angles), jnp.sin(angles)], axis=-1)


def rope_tables(grid_pos):
    quarter = HD // 4
    frequency = jnp.exp(-math.log(10000.0) * jnp.arange(quarter, dtype=F32) / quarter)
    row = frequency[:, None] * grid_pos[:, 0, :].astype(F32).reshape(1, -1)
    col = frequency[:, None] * grid_pos[:, 1, :].astype(F32).reshape(1, -1)
    nil = jnp.zeros_like(row)
    cos_row, sin_row, cos_col, sin_col = jnp.cos(row), jnp.sin(row), jnp.cos(col), jnp.sin(col)
    own = jnp.concatenate([cos_row, cos_row, cos_col, cos_col], axis=0)
    upper = jnp.concatenate([-sin_row, nil, -sin_col, nil], axis=0)
    lower = jnp.concatenate([nil, sin_row, nil, sin_col], axis=0)
    return own, upper, lower


def qkv_norm_kernel(raw_ref, gain_ref, own_ref, upper_ref, lower_ref, out_ref):
    quarter = HD // 4
    for i in range(raw_ref.shape[1]):
        for kind in range(2):
            raw = raw_ref[kind, i]
            mean, rstd = norm_stats(raw, 0)
            value = (raw - mean) * rstd * gain_ref[kind]
            value = (
                value * own_ref[...]
                + pltpu.roll(value, HD - quarter, 0) * upper_ref[...]
                + pltpu.roll(value, quarter, 0) * lower_ref[...]
            )
            out_ref[0, i, kind] = value.astype(BF)
        out_ref[0, i, 2] = raw_ref[2, i].astype(BF)


def qkv_norm_back_kernel(
    grad_ref, raw_ref, gain_ref, own_ref, upper_ref, lower_ref, out_ref, sum_ref
):
    quarter = HD // 4

    @pl.when(pl.program_id(0) == 0)
    def _():
        sum_ref[...] = jnp.zeros_like(sum_ref)

    for i in range(raw_ref.shape[1]):
        for kind in range(2):
            grad = grad_ref[0, i, kind].astype(F32)
            grad = (
                grad * own_ref[...]
                + pltpu.roll(grad * upper_ref[...], quarter, 0)
                + pltpu.roll(grad * lower_ref[...], HD - quarter, 0)
            )
            raw = raw_ref[kind, i]
            mean, rstd = norm_stats(raw, 0)
            back, part = norm_back(grad, raw, mean, rstd, gain_ref[kind], 0)
            out_ref[kind, i] = back.astype(BF)
            sum_ref[kind] += jnp.sum(part, axis=1, keepdims=True)
        out_ref[2, i] = grad_ref[0, i, 2]


def qkv_norm_call(grads, raw, gains, tables, groups, name):
    kinds, heads, features, tokens = raw.shape
    own = heads // groups
    by_kind = pl.BlockSpec((kinds, own, features, tokens), lambda i: (0, i, 0, 0))
    by_group = pl.BlockSpec((1, own, kinds, features, tokens), lambda i: (i, 0, 0, 0, 0))
    table = pl.BlockSpec((features, tokens), lambda i: (0, 0))
    column = pl.BlockSpec((2, features, 1), lambda i: (0, 0, 0))
    group_shape = jax.ShapeDtypeStruct((groups, own, kinds, features, tokens), BF)
    kind_shape = jax.ShapeDtypeStruct(raw.shape, BF)
    total = jax.ShapeDtypeStruct((2, features, 1), F32)
    back = grads is not None
    return pl.pallas_call(
        qkv_norm_back_kernel if back else qkv_norm_kernel,
        grid=(groups,),
        in_specs=([by_group] if back else []) + [by_kind, column] + [table] * 3,
        out_specs=[by_kind, column] if back else by_group,
        out_shape=[kind_shape, total] if back else group_shape,
        compiler_params=pltpu.CompilerParams(vmem_limit_bytes=32 * 2**20),
        cost_estimate=SMALL,
        name=name,
    )(*([grads] if back else []), raw, gains, *tables)


def gate(value):
    corner = value[(0,) * value.ndim].astype(F32)
    return jnp.where(corner != corner, 1.0, 0.0)


def pin_of(*values):
    return jnp.zeros((8, 128), F32) + sum(gate(value) for value in values)


def assemble_kernel(count, moves, starts, *refs):
    pieces, out, sems = refs[:count], refs[count], refs[count + 1]
    copies = [
        pltpu.make_async_copy(
            pieces[piece].at[pl.ds(source, size)],
            out.at[pl.ds(pl.multiple_of(starts[i], 16), size)],
            sems.at[i],
        )
        for i, (piece, source, size) in enumerate(moves)
    ]
    for copy in copies:
        copy.start()
    for copy in copies:
        copy.wait()


def assemble(pieces, moves, starts, rows):
    columns, dtype = pieces[0].shape[1], pieces[0].dtype
    if columns % 128 or any(source % 16 or size % 16 for _, source, size in moves):
        full = jnp.zeros((rows, columns), dtype)
        for (piece, source, size), start in zip(moves, starts):
            block = pieces[piece][source : source + size]
            full = lax.dynamic_update_slice_in_dim(full, block, start, axis=0)
        return full
    count = len(pieces)
    anywhere = pl.BlockSpec(memory_space=pl.ANY)

    def kernel(starts_ref, *refs):
        assemble_kernel(count, moves, starts_ref, *refs)

    return pl.pallas_call(
        kernel,
        out_shape=jax.ShapeDtypeStruct((rows, columns), dtype),
        grid_spec=pltpu.PrefetchScalarGridSpec(
            num_scalar_prefetch=1,
            grid=(1,),
            in_specs=[anywhere] * count,
            out_specs=pl.BlockSpec(memory_space=pltpu.VMEM),
            scratch_shapes=[pltpu.SemaphoreType.DMA((len(moves),))],
        ),
        compiler_params=pltpu.CompilerParams(vmem_limit_bytes=32 * 2**20),
        cost_estimate=SMALL,
        name="assemble",
    )(jnp.stack([jnp.asarray(start, jnp.int32) for start in starts]), *pieces)


def wide(ref, kind, first, count):
    return jnp.concatenate([ref[first + i, 0, kind] for i in range(count)], axis=1)


def contract(left, right, left_dim, right_dim):
    return lax.dot_general(
        left, right, (((left_dim,), (right_dim,)), ((), ())), preferred_element_type=F32
    )


def attend_forward_kernel(step, qkv_ref, pin_ref, out_ref, log_ref):
    blocks, lanes = qkv_ref.shape[0], qkv_ref.shape[4]
    k, v = wide(qkv_ref, 1, 0, blocks), wide(qkv_ref, 2, 0, blocks)
    for first in range(0, blocks, step):
        q = wide(qkv_ref, 0, first, step)
        scores = SCALE * contract(k, q, 0, 0)
        top = jnp.max(scores, axis=0, keepdims=True)
        weights = jnp.exp(scores - top)
        total = jnp.sum(weights, axis=0, keepdims=True)
        out = contract(v, weights.astype(BF), 1, 0) / total
        log_ref[0, 0, :, first * lanes : (first + step) * lanes] = top + jnp.log(total)
        for i in range(step):
            out_ref[first + i, 0, 0] = out[:, i * lanes : (i + 1) * lanes].astype(BF)


def attend_backward_kernel(step, qkv_ref, log_ref, g_ref, pin_ref, out_ref):
    blocks, lanes = qkv_ref.shape[0], qkv_ref.shape[4]
    k, v = wide(qkv_ref, 1, 0, blocks), wide(qkv_ref, 2, 0, blocks)
    dk = jnp.zeros((k.shape[0], k.shape[1]), F32)
    dv = dk
    for first in range(0, blocks, step):
        q, g = wide(qkv_ref, 0, first, step), wide(g_ref, 0, first, step)
        log_sum = log_ref[0, 0, :, first * lanes : (first + step) * lanes]
        probs = jnp.exp(SCALE * contract(k, q, 0, 0) - log_sum)
        grad_probs = contract(v, g, 0, 0)
        delta = jnp.sum(grad_probs * probs, axis=0, keepdims=True)
        grad_scores = (probs * (grad_probs - delta)).astype(BF)
        dq = SCALE * contract(k, grad_scores, 1, 0)
        dk = dk + contract(q, grad_scores, 1, 1)
        dv = dv + contract(g, probs.astype(BF), 1, 1)
        for i in range(step):
            out_ref[first + i, 0, 0] = dq[:, i * lanes : (i + 1) * lanes].astype(BF)
    for i in range(blocks):
        out_ref[i, 0, 1] = (SCALE * dk[:, i * lanes : (i + 1) * lanes]).astype(BF)
        out_ref[i, 0, 2] = dv[:, i * lanes : (i + 1) * lanes].astype(BF)


def attention_call(kernel, arrays, batch, made, name, pin):
    blocks, heads, _, _, lanes = arrays[0].shape
    lanes //= batch

    def spec(kinds):
        if kinds:
            return pl.BlockSpec((blocks, 1, kinds, HD, lanes), lambda b, h: (0, h, 0, 0, b))
        return pl.BlockSpec((1, 1, 1, blocks * lanes), lambda b, h: (b, h, 0, 0))

    def shape(kinds):
        if kinds:
            return jax.ShapeDtypeStruct((blocks, heads, kinds, HD, batch * lanes), BF)
        return jax.ShapeDtypeStruct((batch, heads, 1, blocks * lanes), F32)

    step = max(1, min(blocks, 256 // lanes))
    body = lambda *refs: kernel(step, *refs)
    return pl.pallas_call(
        body,
        grid=(batch, heads),
        in_specs=[spec(a.shape[2] if a.ndim == 5 else 0) for a in arrays]
        + [pl.BlockSpec((8, 128), lambda b, h: (0, 0))],
        out_specs=[spec(kinds) for kinds in made],
        out_shape=[shape(kinds) for kinds in made],
        compiler_params=pltpu.CompilerParams(vmem_limit_bytes=48 * 2**20),
        cost_estimate=SMALL,
        name=name,
    )(*arrays, pin)


def local(
    hidden_in,
    skip_in,
    text_states,
    timesteps,
    positions,
    cotangent,
    skip_gain,
    skip_weight,
    self_norm_gain,
    shift_weight,
    qkv_weight,
    query_gain,
    key_gain,
    self_out_weight,
    cross_norm_gain,
    cross_query_weight,
    text_kv_weight,
    cross_query_gain,
    cross_key_gain,
    cross_out_weight,
    ffn_norm_gain,
    ffn_up_weight,
    ffn_down_weight,
):
    n_dp, n_seq = lax.axis_size("dp"), lax.axis_size(SEQ)
    me_dp, me_x = lax.axis_index("dp"), lax.axis_index("x")
    batch, length, width = hidden_in.shape
    rows = batch * length
    group_heads = H // n_seq
    text_len = text_states.shape[1]


    def dperm(value, mask):
        return lax.ppermute(value, "dp", [(i, i ^ mask) for i in range(n_dp)])

    def xperm(value):
        return lax.ppermute(value, "x", [(0, 1), (1, 0)])

    def zperm(value, mask):
        return lax.ppermute(value, "z", [(i, i ^ mask) for i in range(n_seq // 2)])

    def mixed(value, first, second):
        sizes = {"dp": n_dp, "z": n_seq // 2, "x": 2}

        def number(place):
            return (place["dp"] * sizes["z"] + place["z"]) * 2 + place["x"]

        pairs = []
        for d in range(n_dp):
            for z in range(sizes["z"]):
                for x in range(2):
                    place = {"dp": d, "z": z, "x": x}
                    axis, mask = second if d & 1 else first
                    pairs.append((number(place), number({**place, axis: place[axis] ^ mask})))
        return lax.ppermute(value, ("dp", "z", "x"), pairs)

    core, far_bit = me_dp & 1, (me_dp >> 1) & 1
    z_bit = lax.axis_index("z") & 1
    in_z, in_x, in_far = ("z", 1), ("x", 1), ("dp", 2)

    def by_core(first, second):
        return jnp.where(core == 1, second, first)

    def rows_at(value, start, count):
        return lax.dynamic_slice_in_dim(value, start, count, axis=0)

    def at(value, place):
        return lax.dynamic_index_in_dim(value, place, 0, keepdims=False)

    far_masks = list(range(2, n_dp, 2))

    def held(value, token):
        return (value.astype(F32) + gate(token)).astype(value.dtype)

    def gather_weights(shards, token=None, start=None):
        number, (count, columns) = len(shards), shards[0].shape
        half = count // 2
        shard = jnp.concatenate(shards, axis=0) if number > 1 else shards[0]
        if start is not None:
            shard = held(shard, start)
        pieces, places = [shard, dperm(shard, 1)], [(me_dp, None), (me_dp ^ 1, None)]
        if token is None:
            halves = shard.reshape(number, 2, half, columns)
            mine = by_core(me_x, z_bit)
            part = lax.dynamic_index_in_dim(halves, mine, 1, keepdims=False).reshape(-1, columns)
        for mask in far_masks:
            far, both = me_dp ^ mask, me_dp ^ mask ^ 1
            if token is None:
                near = dperm(part, mask)
                other = mixed(near, in_x, in_z)
                pieces += [near, other, dperm(near, 1), dperm(other, 1)]
                theirs = by_core(z_bit, me_x)
                places += [(far, mine), (far, 1 - mine), (both, theirs), (both, 1 - theirs)]
            else:
                near = held(dperm(shard, mask), token)
                pieces += [near, dperm(near, 1)]
                places += [(far, None), (both, None)]
        gathered, arrived = [], pieces[2]
        for i in range(number):
            moves, starts = [], []
            for j, (owner, which) in enumerate(places):
                size = count if which is None else half
                moves.append((j, i * size, size))
                starts.append(owner * count + (0 if which is None else which * half))
            gathered.append(assemble(pieces, moves, starts, n_dp * count))
        return gathered, arrived

    def split_masks():
        masks, mask = [], n_dp // 2
        while mask:
            masks.append(mask)
            mask //= 2
        return masks

    dp_masks = split_masks()

    def gather_tokens(value, token=None):
        for mask in dp_masks:
            got = dperm(value, mask)
            if token is not None and mask != 1:
                got = held(got, token)
            value = jnp.concatenate([value, got], axis=0)
        return value

    def scatter_tokens(value):
        for mask in reversed(dp_masks):
            half = value.shape[0] // 2
            value = value[:half] + dperm(value[half:].astype(BF), mask).astype(F32)
        return value

    def plus(left, right, *tokens):
        total = left.astype(F32) + right.astype(F32)
        for token in tokens:
            if token is not None:
                total = total + gate(token)
        return total.astype(BF)

    def joined_pair(part, other, axis):
        upper = me_x == 1
        pair = [jnp.where(upper, other, part), jnp.where(upper, part, other)]
        return jnp.concatenate(pair, axis=axis)

    def split_pair(value, axis, which):
        return (
            lax.dynamic_index_in_dim(value, which, axis, keepdims=False),
            lax.dynamic_index_in_dim(value, 1 - which, axis, keepdims=False),
        )

    def quarter_pair(own, token=None):
        pair = jnp.stack([own, mixed(own, in_z, in_x)])
        return pair if token is None else held(pair, token)

    def quarters_in_order(pair, axis):
        stack = jnp.concatenate([pair, mixed(pair, in_x, in_z)], axis=0)
        pieces = []
        for x in range(2):
            for z in range(2):
                rx, rz = me_x ^ x, z_bit ^ z
                pieces.append(at(stack, by_core(2 * rx + rz, 2 * rz + rx)))
        return jnp.concatenate(pieces, axis=axis).astype(F32)

    def far_along_z(value, token):
        mask = 2
        while mask < n_seq // 2:
            value = plus(value, zperm(value, mask), token)
            mask *= 2
        return value

    def shard_sums(blocks):
        number, (_, _, count, columns) = len(blocks), blocks[0].shape

        def side(which):
            size = (n_dp // 2, 1, count, columns)
            picked = [lax.dynamic_slice(b, (0, which, 0, 0), size) for b in blocks]
            return jnp.concatenate(picked, axis=1)

        mine, got = side(core), dperm(side(1 - core), 1)
        token = yield got
        size, mask, bits = n_dp // 2, n_dp // 4, me_dp >> 1
        while size > 2:
            mine, got = plus(mine, got, token), None
            here = bits & mask
            mine = mine.reshape((2, size // 2) + mine.shape[1:])
            keep, send = split_pair(mine, 0, jnp.where(here != 0, 1, 0))
            mine, got = keep, dperm(send, 2 * mask)
            size, mask = size // 2, mask // 2

        def block(which, first, second):
            far = far_bit ^ by_core(first, second)
            x = me_x ^ by_core(second, first)
            begin = (far, 0, x * (count // 2), 0)
            size = (1, number, count // 2, columns)
            return lax.dynamic_slice(which, begin, size)[0]

        def total(first, second):
            return plus(block(mine, first, second), block(got, first, second), token)

        sent = jnp.stack([total(1, 0), total(1, 1)])
        held_back = [total(0, 0), total(0, 1)]
        token = yield sent
        got = mixed(sent, in_far, in_x)
        send = plus(held_back[1], got[1], token)
        own = plus(held_back[0], got[0], token)
        token = yield send
        own = plus(own, mixed(send, in_x, in_far), token)
        size = (number, count // 4, columns)
        keep = lax.dynamic_slice(own, (0, z_bit * (count // 4), 0), size)
        send = lax.dynamic_slice(own, (0, (1 - z_bit) * (count // 4), 0), size)
        token = yield send
        own = plus(keep, zperm(send, 1), token)
        token = yield own
        own = far_along_z(own, token)
        token = yield own
        if token is not None:
            own = held(own, token)
        full = quarters_in_order(quarter_pair(own), 1)
        yield [full[i] for i in range(number)]

    def as_shards(grad):
        return grad.reshape((n_dp // 2, 2, -1) + grad.shape[1:])

    def sum_all(vector):
        for mask in dp_masks:
            vector = vector + dperm(vector, mask)
        vector = vector + xperm(vector)
        mask = 1
        while mask < n_seq // 2:
            vector = vector + zperm(vector, mask)
            mask *= 2
        return vector


    (skip_full,), _ = gather_weights([skip_weight])
    (qkv_full,), _ = gather_weights([qkv_weight])
    text_weight = text_kv_weight.reshape(text_kv_weight.shape[0], -1)
    text_count = text_weight.shape[0]
    text_pieces, text_marks = [text_weight], [0]
    for mask in dp_masks:
        text_pieces = text_pieces + [dperm(piece, mask) for piece in text_pieces]
        text_marks = text_marks + [mark ^ mask for mark in text_marks]
    text_weight = assemble(
        text_pieces,
        [(i, 0, text_count) for i in range(n_dp)],
        [(me_dp ^ mark) * text_count for mark in text_marks],
        n_dp * text_count,
    )
    text_weight = text_weight.reshape((-1,) + text_kv_weight.shape[1:])

    hidden_part = ffn_up_weight.shape[1] // n_dp
    up_rows = ffn_up_weight.shape[0]
    up_blocks = jnp.stack(
        [ffn_up_weight[:, i * hidden_part : (i + 1) * hidden_part] for i in range(n_dp)]
    )
    cot_rows = cotangent.reshape(rows, width)

    def gather_up(token):
        pieces = []
        for mask in range(n_dp):
            block = at(up_blocks, me_dp ^ mask)
            if mask:
                block = dperm(block, mask)
            pieces.append(held(block, token) if mask > 1 else block)
        return pieces[2:], assemble(
            pieces,
            [(i, 0, up_rows) for i in range(n_dp)],
            [(me_dp ^ mask) * up_rows for mask in range(n_dp)],
            n_dp * up_rows,
        )


    text_full = lax.all_gather(text_states, SEQ, axis=2, tiled=True)
    text_kv = jnp.einsum("che,bmc->bhem", text_weight, text_full, preferred_element_type=F32)
    tk_raw = text_kv[:, :, :HD]
    tk_mean, tk_rstd = norm_stats(tk_raw, -2)
    ck_gain = cross_key_gain[:, None]
    tkv_own = jnp.concatenate(
        [((tk_raw - tk_mean) * tk_rstd * ck_gain).astype(BF), text_kv[:, :, HD:].astype(BF)], axis=2
    )
    tkv_all = lax.all_gather(tkv_own, SEQ, axis=1, tiled=True)
    tk_all, tv_all = tkv_all[:, :, :HD], tkv_all[:, :, HD:]


    shift_rows = shift_weight.shape[0]
    all_steps = lax.dynamic_update_slice_in_dim(
        jnp.zeros((n_dp * batch,), F32), timesteps.astype(F32), me_dp * batch, axis=0
    )
    for mask in dp_masks:
        all_steps = all_steps + dperm(all_steps, mask)
    embed_all = jax.nn.silu(time_embed(all_steps, width)).astype(BF)
    embed_part = lax.dynamic_slice_in_dim(embed_all, me_dp * shift_rows, shift_rows, axis=1)
    shift_all = dot(embed_part, shift_weight, 1, 0)

    tables = rope_tables(positions)
    joined = jnp.concatenate([hidden_in, skip_in], axis=-1).reshape(rows, 2 * width).astype(F32)
    skip_mean, skip_rstd = norm_stats(joined, -1)
    skip_bf = ((joined - skip_mean) * skip_rstd * skip_gain).astype(BF)
    x1 = dot(skip_bf, skip_full, 1, 0) + gate(tkv_own)
    one_mean, one_rstd = norm_stats(x1, -1)
    for mask in reversed(dp_masks):
        shift_all = shift_all + dperm(shift_all, mask) + gate(x1)
    shift_vec = rows_at(shift_all, me_dp * batch, batch)
    shift_tokens = jnp.repeat(shift_vec, length, axis=0)
    first_bf = ((x1 - one_mean) * one_rstd * self_norm_gain + shift_tokens).astype(BF)
    qkv_raw = dot(qkv_full, first_bf, 0, 1).reshape(3, H, HD, rows)
    qk_gain = jnp.stack([query_gain, key_gain])[:, :, None]
    direct = length % 128 == 0

    def exchange(value):
        return lax.all_to_all(value, SEQ, split_axis=0, concat_axis=0, tiled=True)

    def to_heads(value):
        kinds = value.shape[2]
        value = exchange(value)
        if not direct:
            value = value.reshape(n_seq, group_heads, kinds, HD, batch, length)
            value = value.transpose(1, 2, 3, 4, 0, 5)
            value = value.reshape(1, group_heads, kinds, HD, batch * n_seq * length)
        return value

    def to_tokens(value):
        kinds = value.shape[2]
        if not direct:
            value = value.reshape(group_heads, kinds, HD, batch, n_seq, length)
            value = value.transpose(4, 0, 1, 2, 3, 5)
            value = value.reshape(n_seq, group_heads, kinds, HD, rows)
        return exchange(value)

    qkv = to_heads(qkv_norm_call(None, qkv_raw, qk_gain, tables, n_seq, "qkv_norm"))
    (self_out_full, cross_query_full, cross_out_full), out_arrived = gather_weights(
        [self_out_weight, cross_query_weight, cross_out_weight], qkv, x1
    )
    out, log_sum = attention_call(
        attend_forward_kernel, [qkv], batch, [1, 0], "attend_forward", pin_of(out_arrived)
    )
    self_tokens = to_tokens(out).reshape(width, rows)
    up_arrived, up_part = gather_up(out)
    cot_all = gather_tokens(cot_rows, self_tokens)
    x2 = x1 + dot(self_tokens, self_out_full, 0, 0) + sum(gate(p) for p in up_arrived)
    two_mean, two_rstd = norm_stats(x2, -1)
    second_bf = ((x2 - two_mean) * two_rstd * cross_norm_gain).astype(BF)

    cq_raw = dot(cross_query_full, second_bf, 0, 1).reshape(H, HD, rows)
    cq_mean, cq_rstd = norm_stats(cq_raw, -2)
    cq_gain = cross_query_gain[:, None]
    cq = ((cq_raw - cq_mean) * cq_rstd * cq_gain).astype(BF).reshape(H, HD, batch, length)
    cross_scores = SCALE * jnp.einsum("hebq,bhem->bhqm", cq, tk_all, preferred_element_type=F32)
    cross_max = jnp.max(cross_scores, axis=-1, keepdims=True)
    cross_exp = jnp.exp(cross_scores - cross_max)
    cross_probs = cross_exp / jnp.sum(cross_exp, axis=-1, keepdims=True)
    cross_probs_bf = cross_probs.astype(BF)
    cross_tokens = (
        jnp.einsum("bhqm,bhem->hebq", cross_probs_bf, tv_all, preferred_element_type=F32)
        .astype(BF)
        .reshape(width, rows)
    )
    x3 = x2 + dot(cross_tokens, cross_out_full, 0, 0)
    three_mean, three_rstd = norm_stats(x3, -1)
    third_bf = ((x3 - three_mean) * three_rstd * ffn_norm_gain).astype(BF)

    third_all = gather_tokens(third_bf)
    up = dot(up_part, third_all, 0, 1)
    active, gelu_pull = jax.vjp(lambda value: jax.nn.gelu(value, approximate=True), up)
    active_bf = active.astype(BF)
    grad_active = dot(ffn_down_weight, cot_all, 1, 1)
    grad_up = gelu_pull(grad_active)[0].astype(BF)
    grad_three_norm = scatter_tokens(dot(grad_up, up_part, 0, 1))
    block_out = x3 + scatter_tokens(dot(active_bf, ffn_down_weight, 0, 0))


    sub = hidden_part // 4

    def hidden_rows(value, first):
        pieces = []
        for second in range(2):
            x, z = me_x ^ by_core(first, second), z_bit ^ by_core(second, first)
            pieces.append(rows_at(value, (2 * x + z) * sub, sub))
        return jnp.concatenate(pieces, axis=0)

    def hidden_sums(left, right):
        sent = dot(hidden_rows(left, 1), right, 1, 0).astype(BF)
        kept = dot(hidden_rows(left, 0), right, 1, 0).astype(BF)
        token = yield sent
        got = mixed(sent, in_x, in_z)
        send = plus(kept[sub:], got[sub:], token)
        own = plus(kept[:sub], got[:sub], token)
        token = yield send
        own = plus(own, mixed(send, in_z, in_x), token)
        token = yield own
        own = far_along_z(own, token)
        token = yield own
        yield own if token is None else held(own, token)

    down = hidden_sums(active_bf, cot_all)
    up_back = hidden_sums(grad_up, third_all)
    first_sent = [next(down), next(up_back)]

    def up_pair(part, token):
        blocks = part.T.reshape(n_dp, up_rows, sub)
        own = [at(blocks, me_dp)] + [dperm(at(blocks, me_dp ^ m), m) for m in range(1, n_dp)]
        own = jnp.stack(own)
        return quarter_pair(jnp.stack([at(own, me_dp ^ i) for i in range(n_dp)]), token)


    grad_three_norm = grad_three_norm + (
        gate(first_sent[0]) + gate(first_sent[1]) + gate(up_back.send(None))
    )
    back_three, ffn_gain_rows = norm_back(
        grad_three_norm, x3, three_mean, three_rstd, ffn_norm_gain, -1
    )
    grad_three = cot_rows.astype(F32) + back_three
    grad_three_bf = grad_three.astype(BF)
    grad_cross = dot(cross_out_full, grad_three_bf, 1, 1).astype(BF).reshape(H, HD, batch, length)
    grad_cprobs = jnp.einsum("hebq,bhem->bhqm", grad_cross, tv_all, preferred_element_type=F32)
    cross_dot = jnp.sum(grad_cprobs * cross_probs, axis=-1, keepdims=True)
    grad_cscores = (cross_probs * (grad_cprobs - cross_dot)).astype(BF)
    grad_cq = (
        SCALE * jnp.einsum("bhqm,bhem->hebq", grad_cscores, tk_all, preferred_element_type=F32)
    ).astype(BF)
    grad_tk = SCALE * jnp.einsum("bhqm,hebq->hbem", grad_cscores, cq, preferred_element_type=F32)
    grad_tv = jnp.einsum("bhqm,hebq->hbem", cross_probs_bf, grad_cross, preferred_element_type=F32)
    grad_tkv = jnp.concatenate([grad_tk, grad_tv], axis=2).astype(BF)
    grad_tkv = grad_tkv.reshape((n_seq // 2, 2, group_heads) + grad_tkv.shape[1:])
    tkv_keep, tkv_send = split_pair(grad_tkv, 1, me_x)
    tkv_got = xperm(tkv_send)

    sent = gate(up_back.send(grad_three_bf)) + gate(down.send(grad_three_bf))
    back_cq, cq_gain_rows = norm_back(
        grad_cq.reshape(H, HD, rows).astype(F32), cq_raw, cq_mean, cq_rstd, cq_gain + sent, -2
    )
    grad_cq_raw = back_cq.astype(BF).reshape(width, rows)
    grad_two_norm = dot(grad_cq_raw, cross_query_full, 0, 1)
    sent = gate(down.send(grad_cq_raw))
    back_two, cross_gain_rows = norm_back(
        grad_two_norm, x2, two_mean, two_rstd, cross_norm_gain + sent, -1
    )
    grad_two = grad_three + back_two
    grad_two_bf = grad_two.astype(BF)
    middle = shard_sums(
        [
            as_shards(dot(cross_tokens, grad_three_bf, 1, 0).astype(BF)),
            as_shards(dot(second_bf, grad_cq_raw, 0, 1).astype(BF)),
            as_shards(dot(self_tokens, grad_two_bf, 1, 0).astype(BF)),
        ]
    )
    next(middle)
    grad_out = dot(self_out_full, grad_two_bf, 1, 1).astype(BF)
    grad_out = to_heads(grad_out.reshape(n_seq, group_heads, 1, HD, rows))
    pin = pin_of(middle.send(grad_two_bf))
    (grad_heads,) = attention_call(
        attend_backward_kernel, [qkv, log_sum, grad_out], batch, [3], "attend_backward", pin
    )
    grad_tokens = to_tokens(grad_heads)
    middle_x = middle.send(grad_heads)
    back_qkv, qk_gain_sum = qkv_norm_call(
        grad_tokens, qkv_raw, qk_gain + gate(middle_x), tables, n_seq, "qkv_norm_back"
    )
    back_qkv = back_qkv.reshape(3 * width, rows)
    late = shard_sums([as_shards(dot(first_bf, back_qkv, 0, 1).astype(BF))])
    next(late)
    grad_one_norm = dot(back_qkv, qkv_full, 0, 1)
    middle_z = middle.send(back_qkv)
    late_far = late.send(back_qkv)
    grad_one_norm = grad_one_norm + (gate(middle_z) + gate(late_far))
    shift_part = jnp.sum(grad_one_norm.reshape(batch, length, width), axis=1)
    back_one, self_gain_rows = norm_back(
        grad_one_norm, x1, one_mean, one_rstd, self_norm_gain, -1
    )
    grad_one_bf = (grad_two + back_one).astype(BF)
    skip_blocks = dot(skip_bf, grad_one_bf, 0, 0).astype(BF)
    skip_blocks = skip_blocks.reshape(n_dp // 2, 2, 2, -1, width)
    end = shard_sums([skip_blocks[:, :, i] for i in range(2)])
    next(end)
    grad_skip_norm = dot(grad_one_bf, skip_full, 1, 1)
    grad_tkv = plus(tkv_keep, tkv_got, grad_one_bf)
    grad_tkv = lax.psum_scatter(grad_tkv, "z", scatter_dimension=0, tiled=True)
    middle_z = middle.send(grad_one_bf)
    end.send(None)
    late.send(grad_one_bf)
    back_joined, skip_gain_rows = norm_back(
        grad_skip_norm, joined, skip_mean, skip_rstd, skip_gain + gate(middle_z), -1
    )
    for half in (down, up_back):
        half.send(grad_one_bf)
    down_pair = quarter_pair(down.send(None))
    up_grad_pair = up_pair(up_back.send(None), None)
    down_grad = quarters_in_order(down_pair, 0)
    up_grad = quarters_in_order(up_grad_pair, 2).transpose(1, 0, 2).reshape(up_rows, -1)
    middle.send(None)
    cross_out_grad, cross_query_grad, self_out_grad = middle.send(None)
    for _ in range(3):
        late.send(None)
    (qkv_grad,) = late.send(None)
    for _ in range(4):
        end.send(None)
    skip_parts = end.send(None)
    skip_grad_w = jnp.concatenate(skip_parts, axis=0)
    back_joined = back_joined.astype(BF).reshape(batch, length, 2 * width)


    grad_tkv = grad_tkv.reshape(grad_tkv.shape[1:]).astype(F32) + gate(grad_one_bf)
    grad_tkv = grad_tkv.swapaxes(0, 1)
    back_tk, ck_gain_rows = norm_back(
        grad_tkv[:, :, :HD], tk_raw, tk_mean, tk_rstd, ck_gain, -2
    )
    grad_tkv_bf = jnp.concatenate([back_tk, grad_tkv[:, :, HD:]], axis=2).astype(BF)
    text_kv_grad = jnp.einsum("bmc,bhem->che", text_full, grad_tkv_bf, preferred_element_type=F32)
    text_part = jnp.einsum("bhem,che->cbm", grad_tkv_bf, text_weight, preferred_element_type=F32)
    text_part = text_part.astype(BF).reshape(n_seq // 2, 2, -1, batch * text_len)
    text_keep, text_send = split_pair(text_part, 1, me_x)
    text_part = plus(text_keep, xperm(text_send))
    text_grad = lax.psum_scatter(text_part, "z", scatter_dimension=0, tiled=True)
    text_grad = text_grad.reshape(-1, batch, text_len).transpose(1, 2, 0)
    text_kv_grad = text_kv_grad.astype(BF).reshape(n_dp // 2, 2, text_count, -1)
    text_keep, text_send = split_pair(text_kv_grad, 1, me_dp & 1)
    text_own = plus(text_keep, dperm(text_send, 1))
    text_kv_sum = at(text_own, me_dp >> 1)
    for mask in far_masks:
        text_kv_sum = plus(text_kv_sum, dperm(at(text_own, (me_dp ^ mask) >> 1), mask))
    text_kv_sum = text_kv_sum.astype(F32).reshape(text_kv_weight.shape)


    shift_slots = lax.dynamic_update_slice_in_dim(
        jnp.zeros((n_dp * batch, width), F32), shift_part, me_dp * batch, axis=0
    )
    vectors = [
        jnp.sum(ffn_gain_rows, axis=0),
        jnp.sum(cross_gain_rows, axis=0),
        jnp.sum(self_gain_rows, axis=0),
        qk_gain_sum[0, :, 0],
        qk_gain_sum[1, :, 0],
        jnp.sum(cq_gain_rows, axis=(0, 2)),
        jnp.sum(ck_gain_rows, axis=(0, 1, 3)),
        shift_slots.reshape(-1),
    ]
    vectors.append(jnp.sum(skip_gain_rows, axis=0))
    total = sum_all(jnp.concatenate(vectors))
    sums, start = [], 0
    for vector in vectors:
        sums.append(total[start : start + vector.shape[0]])
        start += vector.shape[0]
    ffn_gain, cross_gain, self_gain, q_gain_all, k_gain_all, cq_gain_sum, ck_gain_sum = sums[:7]
    shift_total, skip_gain_sum = sums[7:]
    shift_grad = lax.dot_general(
        embed_part.astype(F32),
        shift_total.reshape(n_dp * batch, width),
        (((0,), (0,)), ((), ())),
        precision=lax.Precision.HIGHEST,
        preferred_element_type=F32,
    )

    return (
        block_out.astype(BF).reshape(batch, length, width),
        back_joined[..., :width],
        back_joined[..., width:],
        text_grad,
        skip_gain_sum,
        skip_grad_w,
        self_gain,
        shift_grad,
        qkv_grad,
        q_gain_all,
        k_gain_all,
        self_out_grad,
        cross_gain,
        cross_query_grad,
        text_kv_sum,
        cq_gain_sum,
        ck_gain_sum,
        cross_out_grad,
        ffn_gain,
        up_grad,
        down_grad,
    )


def solution(mesh):
    n_dp, n_seq = mesh.shape["dp"], mesh.shape["seq"]
    mesh = Mesh(mesh.devices.reshape(n_dp, n_seq // 2, 2), ("dp", "z", "x"))
    tokens, text, rows, none = P("dp", SEQ, None), P("dp", None, SEQ), P("dp", None), P()
    heads = P("dp", SEQ, None)
    placed = (
        tokens, tokens, text, P("dp"), text, tokens, none, rows, none, rows, rows, none, none,
        rows, none, rows, heads, none, none, rows, none, rows, rows,
    )
    given = (
        tokens, tokens, tokens, text, none, rows, none, rows, rows, none, none, rows, none, rows,
        heads, none, none, rows, none, rows, rows,
    )
    return jax.shard_map(local, mesh=mesh, in_specs=placed, out_specs=given, check_vma=False)
```

time: 2050 us -> 1120 us (0.55)
  waiting for transfers between devices: 1420 us -> 448 us
  blocking collectives: 122 us -> 0 us
  starting transfers between devices: 30.4 us -> 123 us
  matrix products: 224 us -> 136 us
  other arithmetic: 68.1 us -> 154 us
  Pallas kernels: 0 us -> 61.5 us
  local copies, waits for them, and re-layouts: 164 us -> 129 us
  between operations: 16.4 us -> 48.6 us
    psum x1 -> x0, waiting for transfers between devices: 484 us -> none  [local(): lax.psum(skip_sum.astype(jnp.bfloat16), 'seq').astype(jnp.float32)]
    reduce_scatter x9 -> x2, waiting for transfers between devices: 435 us -> 0.01 us  [the longest x1 0.01 us: local(): grad_tkv = lax.psum_scatter(grad_tkv, 'z', scatter_dimension=0, tiled=True)]
    ppermute x0 -> x74, waiting for transfers between devices: none -> 389 us  [the longest x22 162 us: mixed(): return lax.ppermute(value, ('dp', 'z', 'x'), pairs)]
    all_gather x9 -> x2, waiting for transfers between devices: 263 us -> 0.02 us  [the longest x1 0.02 us: local(): tkv_all = lax.all_gather(tkv_own, SEQ, axis=1, tiled=True)]
    ppermute x0 -> x74, starting transfers between devices: none -> 103 us  [the longest x39 54.4 us: dperm(): return lax.ppermute(value, 'dp', [(i, i ^ mask) for i in range(n_dp)])]
    all_to_all x6 -> x4, waiting for transfers between devices: 161 us -> 58.5 us  [exchange(): return lax.all_to_all(value, SEQ, split_axis=0, concat_axis=0, tiled=True)]
    dot_general x54 -> x34, matrix products: 224 us -> 136 us  [the longest x24 111 us: dot(): lax.dot_general(left, right, (((left_dim,), (right_dim,)), ((), ())), pre...]
    unnamed x21 -> x4, waiting for transfers between devices: 71.9 us -> 0.07 us
  transfers between devices with their start and end apart: 26 -> 82, of which waited for: 18 -> 31; matrix products, arithmetic and copies ran while one was open for 18% -> 28% of each run, Pallas kernels for 0% -> 2%
where the time goes in v1:
time: 1120 us; the launch traced here: 1100 us
  waiting for transfers between devices  448 us (40%)
  other arithmetic  154 us (14%)
  matrix products  136 us (12%)
  local copies, waits for them, and re-layouts  129 us (12%)
  starting transfers between devices  123 us (11%)
  Pallas kernels  61.5 us (5%)
  between operations  48.6 us (4%)
    ppermute x22, waiting for transfers between devices, mixed(): return lax.ppermute(value, ('dp', 'z', 'x'), pairs)  162 us
    dot_general x24, matrix products, dot(): lax.dot_general(left, right, (((left_dim,), (right_dim,)), ((), ())), pre...  111 us
    ppermute x10, waiting for transfers between devices, zperm(): return lax.ppermute(value, 'z', [(i, i ^ mask) for i in range(n_seq // 2)])  110 us
    ppermute x39, waiting for transfers between devices, dperm(): return lax.ppermute(value, 'dp', [(i, i ^ mask) for i in range(n_dp)])  102 us
    convert_element_type x24, other arithmetic, plus(): return total.astype(BF)  59.5 us
    all_to_all x4, waiting for transfers between devices, exchange(): return lax.all_to_all(value, SEQ, split_axis=0, concat_axis=0, tiled=True)  58.5 us
    ppermute x39, starting transfers between devices, dperm(): return lax.ppermute(value, 'dp', [(i, i ^ mask) for i in range(n_dp)])  54.4 us
    pallas_call x2, Pallas kernels, attention_call(): pl.pallas_call(body, grid=(batch, heads), in_specs=[spec(a.shape[2] if a....  31.2 us
  transfers between devices with their start and end apart: 82, of which 31 were waited for; matrix products, arithmetic and copies ran while one was open for 28% of the time, Pallas kernels for 2%

profile of v1, /device:TPU:1, one launch (start us, length us, event | category | flops | bytes accessed | tf_op | source)
XLA Modules:
  0.0 1100.1 jit_solution(4214908861289216376)
XLA Ops:
  26.9 11.4 %collective-permute-done.1.refs_2_ = bf16[352,1408]{1,0:T(8,128)(2,1)} collective-permute-done((bf16[352,1408]{1,0:T(8,128)(2,1)}, bf16[352,1408]{1,0:T(8,128)(2,1)}, u32[]{:S(2)}, u32[]{:S(2)}) %collective-permute-start.1) | collective-permute-done | bytes 991264 | tf_op jit(solution)/shard_map/ppermute | solution.py:290
  46.6 23.5 %collective-permute-done.9.refs_2_ = bf16[176,4224]{1,0:T(8,128)(2,1)} collective-permute-done((bf16[176,4224]{1,0:T(8,128)(2,1)}, bf16[176,4224]{1,0:T(8,128)(2,1)}, u32[]{:S(2)}, u32[]{:S(2)}) %collective-permute-start.9) | collective-permute-done | bytes 1486880 | tf_op jit(solution)/shard_map/ppermute | solution.py:290
  99.4 8.5 assemble.7
  108.0 6.8 fusion.157
  138.4 54.5 %all-to-all-done.refs_0_ = bf16[8,2,3,88,256]{4,3,2,1,0:T(8,128)(2,1)} async-done(((bf16[8,2,3,88,256]{4,3,2,1,0:T(8,128)(2,1)}), bf16[8,2,3,88,256]{4,3,2,1,0:T(8,128)(2,1)}, u32[]{:S(2)}, u32[]{:S(2)}) %all-to-all-start) | async-done | bytes 2162720 | tf_op jit(solution)/shard_map/all_to_all | solution.py:565
  212.3 13.3 %attend_forward.1 = (bf16[8,2,1,88,256]{4,3,2,1,0:T(8,128)(2,1)}, f32[2,2,1,1024]{3,2,1,0:T(1,128)S(1)}) custom-call(bf16[8,2,3,88,256]{4,3,2,1,0:T(8,128)(2,1)} %all-to-all-done.refs_0_, f32[8,128]{1,0:T(8,128)S(1)} %add.923.refs_1_), custom_call_target="tpu_custom_call" | custom-call | flops 1024 | bytes 1024 | tf_op jit(solution)/shard_map/attend_forward/pallas_call | solution.py:243
  238.9 18.0 %collective-permute-done.20 = bf16[352,1536]{1,0:T(8,128)(2,1)} collective-permute-done((bf16[352,1536]{1,0:T(8,128)(2,1)}, bf16[352,1536]{1,0:T(8,128)(2,1)}, u32[]{:S(2)}, u32[]{:S(2)}) %collective-permute-start.20) | collective-permute-done | bytes 1081376 | tf_op jit(solution)/shard_map/ppermute | solution.py:290
  306.3 13.8 %collective-permute-done.23 = bf16[256,1408]{1,0:T(8,128)(2,1)S(1)} collective-permute-done((bf16[256,1408]{1,0:T(8,128)(2,1)S(1)}, bf16[256,1408]{1,0:T(8,128)(2,1)S(1)}, u32[]{:S(2)}, u32[]{:S(2)}) %collective-permute-start.23) | collective-permute-done | bytes 720928 | tf_op jit(solution)/shard_map/ppermute | solution.py:290
  329.4 6.3 collective-permute-done.27
  340.4 9.9 multiply_convert_fusion
  350.4 12.8 %fusion.8 = bf16[1536,1024]{1,0:T(8,128)(2,1)S(1)} fusion(f32[1536,1024]{1,0:T(8,128)} %get-tuple-element.250, bf16[1536,1408]{1,0:T(8,128)(2,1)S(1)} %bitcast.494, bf16[512,1408]{1,0:T(8,128)(2,1)S(1)} %collective-permute-done.28, bf16[256,1408]{1,0:T(8,128)(2,1)S(1)} %add_convert_fusion.31, bf16[256,1408]{1,0:T(8,128)(2,1)} %bitcast.53), kind=kOutput, calls=%fused_computation.16 | convolution fusion | flops 4469293056 | bytes 16646144 | tf_op jit(solution)/shard_map/dot_general | solution.py:21
  406.9 10.5 collective-permute-done.30
  418.6 14.1 %collective-permute-done.26 = bf16[256,1408]{1,0:T(8,128)(2,1)S(1)} collective-permute-done((bf16[256,1408]{1,0:T(8,128)(2,1)S(1)}, bf16[256,1408]{1,0:T(8,128)(2,1)S(1)}, u32[]{:S(2)}, u32[]{:S(2)}) %collective-permute-start.26) | collective-permute-done | bytes 720928 | tf_op jit(solution)/shard_map/ppermute | solution.py:290
  519.0 17.9 %attend_backward.1 = bf16[8,2,3,88,256]{4,3,2,1,0:T(8,128)(2,1)} custom-call(bf16[8,2,3,88,256]{4,3,2,1,0:T(8,128)(2,1)} %all-to-all-done.refs_0_, f32[2,2,1,1024]{3,2,1,0:T(1,128)S(1)} %get-tuple-element.26.refs_1_, bf16[8,2,1,88,256]{4,3,2,1,0:T(8,128)(2,1)S(1)} %all-to-all-done.2.refs_2_, f32[8,128]{1,0:T(8,128)S(1)} %add.990.refs_3_), custom_call_target="tpu_custom_call" | custom-call | flops 1024 | bytes 1024 | tf_op jit(solution)/shard_map/attend_backward/pallas_call | solution.py:243
  549.8 49.8 %collective-permute-done.36 = bf16[2,3,176,1408]{3,2,0,1:T(8,128)(2,1)} collective-permute-done((bf16[2,3,176,1408]{3,2,0,1:T(8,128)(2,1)}, bf16[2,3,176,1408]{3,2,0,1:T(8,128)(2,1)}, u32[]{:S(2)}, u32[]{:S(2)}) %collective-permute-start.36) | collective-permute-done | bytes 2973728 | tf_op jit(solution)/shard_map/ppermute | solution.py:311
  612.6 7.8 convolution_convert_fusion
  660.3 9.3 multiply_reduce_fusion.7
  672.6 26.5 %collective-permute-done.39 = bf16[3,88,1408]{2,1,0:T(8,128)(2,1)} collective-permute-done((bf16[3,88,1408]{2,1,0:T(8,128)(2,1)}, bf16[3,88,1408]{2,1,0:T(8,128)(2,1)}, u32[]{:S(2)}, u32[]{:S(2)}) %collective-permute-start.39) | collective-permute-done | bytes 743456 | tf_op jit(solution)/shard_map/ppermute | solution.py:296
  734.4 19.3 %collective-permute-start.66 = (bf16[352,384]{1,0:T(8,128)(2,1)}, bf16[352,384]{1,0:T(8,128)(2,1)}, u32[]{:S(2)}, u32[]{:S(2)}) collective-permute-start(bf16[352,384]{1,0:T(8,128)(2,1)} %get-tuple-element.214), channel_id=1, source_target_pairs={{0,8},{8,0},{16,24},{24,16},{1,9},{9,1},{17,25},{25,17},{2,10},{10... | collective-permute-start | bytes 811016 | tf_op jit(solution)/shard_map/ppermute | solution.py:290
  769.6 12.6 %collective-permute-done.60 = bf16[3,88,1408]{2,1,0:T(8,128)(2,1)} collective-permute-done((bf16[3,88,1408]{2,1,0:T(8,128)(2,1)}, bf16[3,88,1408]{2,1,0:T(8,128)(2,1)}, u32[]{:S(2)}, u32[]{:S(2)}) %collective-permute-start.60) | collective-permute-done | bytes 743456 | tf_op jit(solution)/shard_map/ppermute | solution.py:296
  790.8 23.7 %collective-permute-done.61 = bf16[3,88,1408]{2,1,0:T(8,128)(2,1)S(1)} collective-permute-done((bf16[3,88,1408]{2,1,0:T(8,128)(2,1)S(1)}, bf16[3,88,1408]{2,1,0:T(8,128)(2,1)S(1)}, u32[]{:S(2)}, u32[]{:S(2)}) %collective-permute-start.61) | collective-permute-done | bytes 743456 | tf_op jit(solution)/shard_map/ppermute | solution.py:311
  816.4 12.6 %collective-permute-done.69 = bf16[4,352,384]{2,1,0:T(8,128)(2,1)S(1)} collective-permute-done((bf16[4,352,384]{2,1,0:T(8,128)(2,1)S(1)}, bf16[4,352,384]{2,1,0:T(8,128)(2,1)S(1)}, u32[]{:S(2)}, u32[]{:S(2)}) %collective-permute-start.69) | collective-permute-done | bytes 1081376 | tf_op jit(solution)/shard_map/ppermute | solution.py:311
  835.8 9.5 collective-permute-done.62
  849.0 19.4 %collective-permute-done.73 = bf16[2,384,1408]{2,1,0:T(8,128)(2,1)S(1)} collective-permute-done((bf16[2,384,1408]{2,1,0:T(8,128)(2,1)S(1)}, bf16[2,384,1408]{2,1,0:T(8,128)(2,1)S(1)}, u32[]{:S(2)}, u32[]{:S(2)}) %collective-permute-start.73) | collective-permute-done | bytes 2162720 | tf_op jit(solution)/shard_map/ppermute | solution.py:311
  869.3 8.7 maximum_convert_fusion
  878.1 13.6 %collective-permute-done.70 = bf16[2,4,352,384]{3,2,1,0:T(8,128)(2,1)S(1)} collective-permute-done((bf16[2,4,352,384]{3,2,1,0:T(8,128)(2,1)S(1)}, bf16[2,4,352,384]{3,2,1,0:T(8,128)(2,1)S(1)}, u32[]{:S(2)}, u32[]{:S(2)}) %collective-permute-start.70) | collective-permute-done | bytes 2162720 | tf_op jit(solution)/shard_map/ppermute | solution.py:311
  920.9 15.0 %collective-permute-done.44 = f32[18656]{0:T(1024)S(1)} collective-permute-done((f32[18656]{0:T(1024)S(1)}, f32[18656]{0:T(1024)S(1)}, u32[]{:S(2)}, u32[]{:S(2)}) %collective-permute-start.44) | collective-permute-done | bytes 74656 | tf_op jit(solution)/shard_map/ppermute | solution.py:293
  949.4 9.1 collective-permute-done.46
  974.7 36.0 %collective-permute-done.57 = bf16[1,88,4224]{2,1,0:T(8,128)(2,1)S(1)} collective-permute-done((bf16[1,88,4224]{2,1,0:T(8,128)(2,1)}, bf16[1,88,4224]{2,1,0:T(8,128)(2,1)S(1)}, u32[]{:S(2)}, u32[]{:S(2)}) %collective-permute-start.57) | collective-permute-done | bytes 743456 | tf_op jit(solution)/shard_map/ppermute | solution.py:296
  1040.1 21.3 %collective-permute-done.51 = bf16[2,88,1408]{2,1,0:T(8,128)(2,1)} collective-permute-done((bf16[2,88,1408]{2,1,0:T(8,128)(2,1)S(1)}, bf16[2,88,1408]{2,1,0:T(8,128)(2,1)}, u32[]{:S(2)}, u32[]{:S(2)}) %collective-permute-start.51) | collective-permute-done | bytes 495648 | tf_op jit(solution)/shard_map/ppermute | solution.py:296
  1063.6 6.8 collective-permute-done.52
  1078.9 11.0 collective-permute-done.53
  (699 shorter events, 518.1 us)
Async XLA Ops:
  7.2 68.2 %all-gather.3.cloned.1.call-start = ((), (), s32[]{:S(2)}) async-start(), calls=%async_computation.6 | async-start | bytes 1548288 | tf_op jit(solution)/shard_map/all_gather | solution.py:527
  18.9 51.1 %collective-permute-start.9 = (bf16[176,4224]{1,0:T(8,128)(2,1)}, bf16[176,4224]{1,0:T(8,128)(2,1)}, u32[]{:S(2)}, u32[]{:S(2)}) collective-permute-start(bf16[176,4224]{1,0:T(8,128)(2,1)} %dynamic-slice_bitcast_fusion.4), channel_id=1, source_target_pairs={{0,16},{8,24},{16,0},{24,8},{1,17},{9,25},{17,1},{25,9},{2,18},{10... | collective-permute-start | bytes 4460552 | tf_op jit(solution)/shard_map/ppermute | solution.py:290
  46.3 53.0 %collective-permute-start.8 = (bf16[352,4224]{1,0:T(8,128)(2,1)}, bf16[352,4224]{1,0:T(8,128)(2,1)}, u32[]{:S(2)}, u32[]{:S(2)}) collective-permute-start(bf16[352,4224]{1,0:T(8,128)(2,1)} %refs_0_.3), channel_id=1, source_target_pairs={{0,8},{8,0},{16,24},{24,16},{1,9},{9,1},{17,25},{25,17},{2,10},{10... | collective-permute-start | bytes 8921096 | tf_op jit(solution)/shard_map/ppermute | solution.py:290
  121.1 71.8 %all-to-all-start = ((bf16[8,2,3,88,256]{4,3,2,1,0:T(8,128)(2,1)}), bf16[8,2,3,88,256]{4,3,2,1,0:T(8,128)(2,1)}, u32[]{:S(2)}, u32[]{:S(2)}) async-start(bf16[8,2,3,88,256]{4,3,2,1,0:T(8,128)(2,1)} %qkv_norm.1), calls=%async_computation | async-start | bytes 4325376 | tf_op jit(solution)/shard_map/all_to_all | solution.py:565
  126.8 134.3 %all-gather.5.cloned.1.call-start = ((), (), s32[]{:S(2)}) async-start(), calls=%async_computation.7 | async-start | bytes 4866048 | tf_op jit(solution)/shard_map/all_gather | solution.py:535
  129.5 65.9 %collective-permute-start.17 = (bf16[1056,1408]{1,0:T(8,128)(2,1)S(1)}, bf16[1056,1408]{1,0:T(8,128)(2,1)}, u32[]{:S(2)}, u32[]{:S(2)}) collective-permute-start(bf16[1056,1408]{1,0:T(8,128)(2,1)S(1)} %add_convert_fusion.1.refs_0_), channel_id=1, source_target_pairs={{0,16},{8,24},{16,0},{24,8},{1,17},{9,25},{17,1},{25,9},{2,18},{10... | collective-permute-start | bytes 8921096 | tf_op jit(solution)/shard_map/ppermute | solution.py:290
  137.1 128.8 %collective-permute-start.18 = (bf16[1056,1408]{1,0:T(8,128)(2,1)S(1)}, bf16[1056,1408]{1,0:T(8,128)(2,1)}, u32[]{:S(2)}, u32[]{:S(2)}) collective-permute-start(bf16[1056,1408]{1,0:T(8,128)(2,1)S(1)} %add_convert_fusion.1.refs_0_), channel_id=1, source_target_pairs={{0,8},{8,0},{16,24},{24,16},{1,9},{9,1},{17,25},{25,17},{2,10},{10... | collective-permute-start | bytes 8921096 | tf_op jit(solution)/shard_map/ppermute | solution.py:290
  199.6 66.3 %collective-permute-start.19 = (bf16[1056,1408]{1,0:T(8,128)(2,1)}, bf16[1056,1408]{1,0:T(8,128)(2,1)}, u32[]{:S(2)}, u32[]{:S(2)}) collective-permute-start(bf16[1056,1408]{1,0:T(8,128)(2,1)} %add_convert_fusion.refs_2_), channel_id=1, source_target_pairs={{0,8},{8,0},{16,24},{24,16},{1,9},{9,1},{17,25},{25,17},{2,10},{10... | collective-permute-start | bytes 8921096 | tf_op jit(solution)/shard_map/ppermute | solution.py:290
  209.4 47.5 %collective-permute-start.20 = (bf16[352,1536]{1,0:T(8,128)(2,1)}, bf16[352,1536]{1,0:T(8,128)(2,1)}, u32[]{:S(2)}, u32[]{:S(2)}) collective-permute-start(bf16[352,1536]{1,0:T(8,128)(2,1)} %get-tuple-element.163), channel_id=1, source_target_pairs={{0,16},{8,24},{16,0},{24,8},{1,17},{9,25},{17,1},{25,9},{2,18},{10... | collective-permute-start | bytes 3244040 | tf_op jit(solution)/shard_map/ppermute | solution.py:290
  226.7 43.8 %all-to-all-start.1 = ((bf16[8,2,1,88,256]{4,3,2,1,0:T(8,128)(2,1)}), bf16[8,2,1,88,256]{4,3,2,1,0:T(8,128)(2,1)}, u32[]{:S(2)}, u32[]{:S(2)}) async-start(bf16[8,2,1,88,256]{4,3,2,1,0:T(8,128)(2,1)} %get-tuple-element.25), calls=%async_computation.1 | async-start | bytes 1441792 | tf_op jit(solution)/shard_map/all_to_all | solution.py:565
  381.3 59.0 %collective-permute-start.33 = (bf16[768,1408]{1,0:T(8,128)(2,1)}, bf16[768,1408]{1,0:T(8,128)(2,1)S(1)}, u32[]{:S(2)}, u32[]{:S(2)}) collective-permute-start(bf16[768,1408]{1,0:T(8,128)(2,1)} %convolution_convert_fusion.8), channel_id=1, source_target_pairs={{0,1},{1,0},{2,3},{3,2},{4,5},{5,4},{6,7},{7,6},{8,10},{9,11},{10,... | collective-permute-start | bytes 6488072 | tf_op jit(solution)/shard_map/ppermute | solution.py:311
  404.4 54.3 %collective-permute-start.32 = (bf16[384,1408]{1,0:T(8,128)(2,1)}, bf16[384,1408]{1,0:T(8,128)(2,1)}, u32[]{:S(2)}, u32[]{:S(2)}) collective-permute-start(bf16[384,1408]{1,0:T(8,128)(2,1)} %add_convert_fusion.17), channel_id=1, source_target_pairs={{0,2},{1,3},{2,0},{3,1},{4,6},{5,7},{6,4},{7,5},{8,9},{9,8},{10,11... | collective-permute-start | bytes 3244040 | tf_op jit(solution)/shard_map/ppermute | solution.py:311
  536.9 69.5 %all-to-all-start.3 = ((bf16[8,2,3,88,256]{4,3,2,1,0:T(8,128)(2,1)}), bf16[8,2,3,88,256]{4,3,2,1,0:T(8,128)(2,1)S(1)}, u32[]{:S(2)}, u32[]{:S(2)}) async-start(bf16[8,2,3,88,256]{4,3,2,1,0:T(8,128)(2,1)} %attend_backward.1), calls=%async_computation.3 | async-start | bytes 4325376 | tf_op jit(solution)/shard_map/all_to_all | solution.py:565
  541.9 356.5 %reduce-scatter.3.cloned.1.call-start = ((), (), s32[]{:S(2)}) async-start(), calls=%async_computation.8 | async-start | bytes 2703360 | tf_op jit(solution)/shard_map/reduce_scatter | solution.py:731
  545.7 53.9 %collective-permute-start.36 = (bf16[2,3,176,1408]{3,2,0,1:T(8,128)(2,1)}, bf16[2,3,176,1408]{3,2,0,1:T(8,128)(2,1)}, u32[]{:S(2)}, u32[]{:S(2)}) collective-permute-start(bf16[2,3,176,1408]{3,2,0,1:T(8,128)(2,1)} %pad_maximum_fusion.7), channel_id=1, source_target_pairs={{0,16},{1,17},{2,18},{3,19},{4,20},{5,21},{6,22},{7,23},{8,9},{9,8... | collective-permute-start | bytes 8921096 | tf_op jit(solution)/shard_map/ppermute | solution.py:311
  635.1 86.6 %collective-permute-start.40 = (bf16[4,2,2,176,333]{4,3,2,1,0:T(8,128)(2,1)}, bf16[4,2,2,176,333]{4,3,2,1,0:T(8,128)(2,1)}, u32[]{:S(2)}, u32[]{:S(2)}) collective-permute-start(bf16[4,2,2,176,333]{4,3,2,1,0:T(8,128)(2,1)} %fusion.39), channel_id=1, source_target_pairs={{0,1},{1,0},{2,3},{3,2},{4,5},{5,4},{6,7},{7,6},{8,9},{9,8},{10,11... | collective-permute-start | bytes 5626376 | tf_op jit(solution)/shard_map/ppermute | solution.py:293
  635.1 72.1 %collective-permute-start.65 = (bf16[384,1408]{1,0:T(8,128)(2,1)}, bf16[384,1408]{1,0:T(8,128)(2,1)}, u32[]{:S(2)}, u32[]{:S(2)}) collective-permute-start(bf16[384,1408]{1,0:T(8,128)(2,1)} %add_convert_fusion.15), channel_id=1, source_target_pairs={{0,4},{2,6},{4,0},{6,2},{1,5},{3,7},{5,1},{7,3},{8,12},{10,14},{12... | collective-permute-start | bytes 3244040 | tf_op jit(solution)/shard_map/ppermute | solution.py:296
  637.4 122.7 %collective-permute-start.71 = (bf16[384,1408]{1,0:T(8,128)(2,1)}, bf16[384,1408]{1,0:T(8,128)(2,1)}, u32[]{:S(2)}, u32[]{:S(2)}) collective-permute-start(bf16[384,1408]{1,0:T(8,128)(2,1)} %add_convert_fusion.12), channel_id=1, source_target_pairs={{0,4},{2,6},{4,0},{6,2},{1,5},{3,7},{5,1},{7,3},{8,12},{10,14},{12... | collective-permute-start | bytes 3244040 | tf_op jit(solution)/shard_map/ppermute | solution.py:296
  651.1 48.0 %collective-permute-start.39 = (bf16[3,88,1408]{2,1,0:T(8,128)(2,1)}, bf16[3,88,1408]{2,1,0:T(8,128)(2,1)}, u32[]{:S(2)}, u32[]{:S(2)}) collective-permute-start(bf16[3,88,1408]{2,1,0:T(8,128)(2,1)} %constant_dynamic-slice_fusion.11), channel_id=1, source_target_pairs={{0,2},{2,0},{4,6},{6,4},{1,3},{3,1},{5,7},{7,5},{8,10},{10,8},{12,... | collective-permute-start | bytes 2230280 | tf_op jit(solution)/shard_map/ppermute | solution.py:296
  702.5 79.8 %collective-permute-start.60 = (bf16[3,88,1408]{2,1,0:T(8,128)(2,1)}, bf16[3,88,1408]{2,1,0:T(8,128)(2,1)}, u32[]{:S(2)}, u32[]{:S(2)}) collective-permute-start(bf16[3,88,1408]{2,1,0:T(8,128)(2,1)} %add_convert_fusion.29), channel_id=1, source_target_pairs={{0,4},{2,6},{4,0},{6,2},{1,5},{3,7},{5,1},{7,3},{8,12},{10,14},{12... | collective-permute-start | bytes 2230280 | tf_op jit(solution)/shard_map/ppermute | solution.py:296
  726.9 309.9 %reduce-scatter.5.cloned.1.call-start = ((), (), s32[]{:S(2)}) async-start(), calls=%async_computation.9 | async-start | bytes 860160 | tf_op jit(solution)/shard_map/reduce_scatter | solution.py:767
  760.3 69.1 %collective-permute-start.54 = (bf16[2,1,176,4224]{3,2,0,1:T(8,128)(2,1)S(1)}, bf16[2,1,176,4224]{3,2,0,1:T(8,128)(2,1)S(1)}, u32[]{:S(2)}, u32[]{:S(2)}) collective-permute-start(bf16[2,1,176,4224]{3,2,0,1:T(8,128)(2,1)S(1)} %copy-done.78), channel_id=1, source_target_pairs={{0,16},{1,17},{2,18},{3,19},{4,20},{5,21},{6,22},{7,23},{8,9},{9,8... | collective-permute-start | bytes 8921096 | tf_op jit(solution)/shard_map/ppermute | solution.py:311
  767.0 47.7 %collective-permute-start.72 = (bf16[384,1408]{1,0:T(8,128)(2,1)S(1)}, bf16[384,1408]{1,0:T(8,128)(2,1)S(1)}, u32[]{:S(2)}, u32[]{:S(2)}) collective-permute-start(bf16[384,1408]{1,0:T(8,128)(2,1)S(1)} %add_convert_fusion.10), channel_id=1, source_target_pairs={{0,2},{1,3},{2,0},{3,1},{4,6},{5,7},{6,4},{7,5},{8,9},{9,8},{10,11... | collective-permute-start | bytes 3244040 | tf_op jit(solution)/shard_map/ppermute | solution.py:311
  768.4 150.3 %collective-permute-start.47 = (bf16[2,2,352,1408]{3,2,1,0:T(8,128)(2,1)}, bf16[2,2,352,1408]{3,2,1,0:T(8,128)(2,1)}, u32[]{:S(2)}, u32[]{:S(2)}) collective-permute-start(bf16[2,2,352,1408]{3,2,1,0:T(8,128)(2,1)} %pad_maximum_fusion.5), channel_id=1, source_target_pairs={{0,8},{8,0},{16,24},{24,16},{1,9},{9,1},{17,25},{25,17},{2,10},{10... | collective-permute-start | bytes 11894792 | tf_op jit(solution)/shard_map/ppermute | solution.py:290
  789.5 39.6 %collective-permute-start.69 = (bf16[4,352,384]{2,1,0:T(8,128)(2,1)S(1)}, bf16[4,352,384]{2,1,0:T(8,128)(2,1)S(1)}, u32[]{:S(2)}, u32[]{:S(2)}) collective-permute-start(bf16[4,352,384]{2,1,0:T(8,128)(2,1)S(1)} %get-tuple-element.206), channel_id=1, source_target_pairs={{0,2},{1,3},{2,0},{3,1},{4,6},{5,7},{6,4},{7,5},{8,9},{9,8},{10,11... | collective-permute-start | bytes 3244040 | tf_op jit(solution)/shard_map/ppermute | solution.py:311
  814.9 53.5 %collective-permute-start.73 = (bf16[2,384,1408]{2,1,0:T(8,128)(2,1)S(1)}, bf16[2,384,1408]{2,1,0:T(8,128)(2,1)S(1)}, u32[]{:S(2)}, u32[]{:S(2)}) collective-permute-start(bf16[2,384,1408]{2,1,0:T(8,128)(2,1)S(1)} %pad_maximum_fusion.14), channel_id=1, source_target_pairs={{0,1},{1,0},{2,3},{3,2},{4,5},{5,4},{6,7},{7,6},{8,10},{9,11},{10,... | collective-permute-start | bytes 6488072 | tf_op jit(solution)/shard_map/ppermute | solution.py:311
  829.3 62.4 %collective-permute-start.70 = (bf16[2,4,352,384]{3,2,1,0:T(8,128)(2,1)S(1)}, bf16[2,4,352,384]{3,2,1,0:T(8,128)(2,1)S(1)}, u32[]{:S(2)}, u32[]{:S(2)}) collective-permute-start(bf16[2,4,352,384]{3,2,1,0:T(8,128)(2,1)S(1)} %pad_maximum_fusion.13), channel_id=1, source_target_pairs={{0,1},{1,0},{2,3},{3,2},{4,5},{5,4},{6,7},{7,6},{8,10},{9,11},{10,... | collective-permute-start | bytes 6488072 | tf_op jit(solution)/shard_map/ppermute | solution.py:311
  834.5 101.6 %collective-permute-start.55 = (bf16[1,176,4224]{2,1,0:T(8,128)(2,1)}, bf16[1,176,4224]{2,1,0:T(8,128)(2,1)}, u32[]{:S(2)}, u32[]{:S(2)}) collective-permute-start(bf16[1,176,4224]{2,1,0:T(8,128)(2,1)} %fusion.71), channel_id=1, source_target_pairs={{0,1},{1,0},{2,3},{3,2},{4,5},{5,4},{6,7},{7,6},{8,24},{9,25},{10,... | collective-permute-start | bytes 4460552 | tf_op jit(solution)/shard_map/ppermute | solution.py:311
  917.2 51.7 %collective-permute-start.41 = (bf16[4,128,666]{1,0,2:T(4,128)(2,1)}, bf16[4,128,666]{1,0,2:T(4,128)(2,1)}, u32[]{:S(2)}, u32[]{:S(2)}) collective-permute-start(bf16[4,128,666]{1,0,2:T(4,128)(2,1)} %copy.211), channel_id=1, source_target_pairs={{0,1},{1,0},{2,3},{3,2},{4,5},{5,4},{6,7},{7,6},{8,9},{9,8},{10,11... | collective-permute-start | bytes 2045960 | tf_op jit(solution)/shard_map/ppermute | solution.py:293
  948.2 86.8 %collective-permute-start.64 = (bf16[256,352]{0,1:T(8,128)(2,1)}, bf16[256,352]{0,1:T(8,128)(2,1)}, u32[]{:S(2)}, u32[]{:S(2)}) collective-permute-start(bf16[256,352]{0,1:T(8,128)(2,1)} %dynamic-slice_bitcast_fusion.33), channel_id=1, source_target_pairs={{0,16},{8,24},{16,0},{24,8},{1,17},{9,25},{17,1},{25,9},{2,18},{10... | collective-permute-start | bytes 540680 | tf_op jit(solution)/shard_map/ppermute | solution.py:290
  966.0 44.6 %collective-permute-start.57 = (bf16[1,88,4224]{2,1,0:T(8,128)(2,1)}, bf16[1,88,4224]{2,1,0:T(8,128)(2,1)S(1)}, u32[]{:S(2)}, u32[]{:S(2)}) collective-permute-start(bf16[1,88,4224]{2,1,0:T(8,128)(2,1)} %add_convert_fusion.28), channel_id=1, source_target_pairs={{0,4},{2,6},{4,0},{6,2},{1,5},{3,7},{5,1},{7,3},{8,12},{10,14},{12... | collective-permute-start | bytes 2230280 | tf_op jit(solution)/shard_map/ppermute | solution.py:296
  973.4 40.1 %collective-permute-start.49 = (bf16[2,176,1408]{2,1,0:T(8,128)(2,1)S(1)}, bf16[2,176,1408]{2,1,0:T(8,128)(2,1)S(1)}, u32[]{:S(2)}, u32[]{:S(2)}) collective-permute-start(bf16[2,176,1408]{2,1,0:T(8,128)(2,1)S(1)} %fusion.109), channel_id=1, source_target_pairs={{0,1},{1,0},{2,3},{3,2},{4,5},{5,4},{6,7},{7,6},{8,24},{9,25},{10,... | collective-permute-start | bytes 2973704 | tf_op jit(solution)/shard_map/ppermute | solution.py:311
  (187 other events, 2297.4 us)
Sparse Core Ops, SparseCore 0:
  12.6 48.4 all-gather.2
  132.9 99.4 all-gather.4
  727.0 78.7 reduce-scatter.2
  971.4 33.6 reduce-scatter.4

commit v2 on v1

--- a/solution.py
+++ b/solution.py
@@ -406,8 +406,8 @@
         pair = jnp.stack([own, mixed(own, in_z, in_x)])
         return pair if token is None else held(pair, token)
 
-    def quarters_in_order(pair, axis):
-        stack = jnp.concatenate([pair, mixed(pair, in_x, in_z)], axis=0)
+    def quarters_in_order(pair, axis, token):
+        stack = jnp.concatenate([pair, held(mixed(pair, in_x, in_z), token)], axis=0)
         pieces = []
         for x in range(2):
             for z in range(2):
@@ -467,9 +467,9 @@
         token = yield own
         own = far_along_z(own, token)
         token = yield own
-        if token is not None:
-            own = held(own, token)
-        full = quarters_in_order(quarter_pair(own), 1)
+        pair = quarter_pair(own, token)
+        token = yield pair
+        full = quarters_in_order(pair, 1, token)
         yield [full[i] for i in range(number)]
 
     def as_shards(grad):
@@ -507,12 +507,13 @@
     up_blocks = jnp.stack(
         [ffn_up_weight[:, i * hidden_part : (i + 1) * hidden_part] for i in range(n_dp)]
     )
+    up_sends = [at(up_blocks, me_dp ^ mask) for mask in range(n_dp)]
     cot_rows = cotangent.reshape(rows, width)
 
     def gather_up(token):
         pieces = []
         for mask in range(n_dp):
-            block = at(up_blocks, me_dp ^ mask)
+            block = up_sends[mask]
             if mask:
                 block = dperm(block, mask)
             pieces.append(held(block, token) if mask > 1 else block)
@@ -550,7 +551,7 @@
     joined = jnp.concatenate([hidden_in, skip_in], axis=-1).reshape(rows, 2 * width).astype(F32)
     skip_mean, skip_rstd = norm_stats(joined, -1)
     skip_bf = ((joined - skip_mean) * skip_rstd * skip_gain).astype(BF)
-    x1 = dot(skip_bf, skip_full, 1, 0) + gate(tkv_own)
+    x1 = dot(skip_bf, skip_full, 1, 0) + gate(tkv_own) + sum(gate(b) for b in up_sends[1:])
     one_mean, one_rstd = norm_stats(x1, -1)
     for mask in reversed(dp_masks):
         shift_all = shift_all + dperm(shift_all, mask) + gate(x1)
@@ -730,30 +731,49 @@
     grad_tkv = plus(tkv_keep, tkv_got, grad_one_bf)
     grad_tkv = lax.psum_scatter(grad_tkv, "z", scatter_dimension=0, tiled=True)
     middle_z = middle.send(grad_one_bf)
-    end.send(None)
-    late.send(grad_one_bf)
     back_joined, skip_gain_rows = norm_back(
         grad_skip_norm, joined, skip_mean, skip_rstd, skip_gain + gate(middle_z), -1
     )
-    for half in (down, up_back):
-        half.send(grad_one_bf)
-    down_pair = quarter_pair(down.send(None))
-    up_grad_pair = up_pair(up_back.send(None), None)
-    down_grad = quarters_in_order(down_pair, 0)
-    up_grad = quarters_in_order(up_grad_pair, 2).transpose(1, 0, 2).reshape(up_rows, -1)
-    middle.send(None)
-    cross_out_grad, cross_query_grad, self_out_grad = middle.send(None)
-    for _ in range(3):
-        late.send(None)
-    (qkv_grad,) = late.send(None)
-    for _ in range(4):
-        end.send(None)
-    skip_parts = end.send(None)
+
+    steps = [grad_one_bf]
+
+    def then(value):
+        steps.append(value[0] if isinstance(value, list) else value)
+        return value
+
+    def step(sums):
+        return then(sums.send(steps[-1]))
+
+    step(down)
+    down_own = down.send(None)
+    step(end)
+    step(late)
+    down_pair = then(quarter_pair(down_own, steps[-1]))
+    step(up_back)
+    up_own = up_back.send(None)
+    step(end)
+    step(middle)
+    step(late)
+    up_grad_pair = then(up_pair(up_own, steps[-1]))
+    step(end)
+    step(middle)
+    step(late)
+    down_grad = then(quarters_in_order(down_pair, 0, steps[-1]))
+    step(end)
+    up_grad = then(quarters_in_order(up_grad_pair, 2, steps[-1]))
+    up_grad = up_grad.transpose(1, 0, 2).reshape(up_rows, -1)
+    step(late)
+    cross_out_grad, cross_query_grad, self_out_grad = step(middle)
+    step(end)
+    step(late)
+    step(end)
+    (qkv_grad,) = step(late)
+    skip_parts = step(end)
     skip_grad_w = jnp.concatenate(skip_parts, axis=0)
     back_joined = back_joined.astype(BF).reshape(batch, length, 2 * width)
 
 
-    grad_tkv = grad_tkv.reshape(grad_tkv.shape[1:]).astype(F32) + gate(grad_one_bf)
+    grad_tkv = grad_tkv.reshape(grad_tkv.shape[1:]).astype(F32) + gate(steps[8])
     grad_tkv = grad_tkv.swapaxes(0, 1)
     back_tk, ck_gain_rows = norm_back(
         grad_tkv[:, :, :HD], tk_raw, tk_mean, tk_rstd, ck_gain, -2

time: 1120 us -> 1100 us (0.982)
  waiting for transfers between devices: 448 us -> 408 us
  between operations: 48.6 us -> 79.1 us
  starting transfers between devices: 123 us -> 93.8 us
  local copies, waits for them, and re-layouts: 129 us -> 145 us
  other arithmetic: 154 us -> 166 us
    ppermute x22, waiting for transfers between devices: 162 us -> 97.9 us  [mixed(): return lax.ppermute(value, ('dp', 'z', 'x'), pairs)]
    ppermute x10, waiting for transfers between devices: 110 us -> 140 us  [zperm(): return lax.ppermute(value, 'z', [(i, i ^ mask) for i in range(n_seq // 2)])]
    ppermute x39, starting transfers between devices: 54.4 us -> 35.4 us  [dperm(): return lax.ppermute(value, 'dp', [(i, i ^ mask) for i in range(n_dp)])]
    slice x24 -> x46, local copies, waits for them, and re-layouts: 21.2 us -> 37.4 us  [gate(): corner = value[(0,) * value.ndim].astype(F32)]
    convert_element_type x5 -> x15, other arithmetic: 10.7 us -> 23.5 us  [held(): return (value.astype(F32) + gate(token)).astype(value.dtype)]
    unnamed x279 -> x308, local copies, waits for them, and re-layouts: 24.3 us -> 28 us
    convert_element_type x24 -> x25, other arithmetic: 59.5 us -> 57.8 us  [plus(): return total.astype(BF)]
  transfers between devices with their start and end apart: 82 -> 82, of which waited for: 31 -> 25; matrix products, arithmetic and copies ran while one was open for 28% -> 31% of each run, Pallas kernels for 2% -> 2%
where the time goes in v2:
time: 1100 us; the launch traced here: 1090 us
  waiting for transfers between devices  408 us (37%)
  other arithmetic  166 us (15%)
  local copies, waits for them, and re-layouts  145 us (13%)
  matrix products  133 us (12%)
  starting transfers between devices  93.8 us (9%)
  between operations  79.1 us (7%)
  Pallas kernels  61.7 us (6%)
    ppermute x10, waiting for transfers between devices, zperm(): return lax.ppermute(value, 'z', [(i, i ^ mask) for i in range(n_seq // 2)])  140 us
    dot_general x24, matrix products, dot(): lax.dot_general(left, right, (((left_dim,), (right_dim,)), ((), ())), pre...  107 us
    ppermute x22, waiting for transfers between devices, mixed(): return lax.ppermute(value, ('dp', 'z', 'x'), pairs)  97.9 us
    ppermute x39, waiting for transfers between devices, dperm(): return lax.ppermute(value, 'dp', [(i, i ^ mask) for i in range(n_dp)])  95.5 us
    all_to_all x4, waiting for transfers between devices, exchange(): return lax.all_to_all(value, SEQ, split_axis=0, concat_axis=0, tiled=True)  62.6 us
    convert_element_type x25, other arithmetic, plus(): return total.astype(BF)  57.8 us
    slice x46, local copies, waits for them, and re-layouts, gate(): corner = value[(0,) * value.ndim].astype(F32)  37.4 us
    ppermute x39, starting transfers between devices, dperm(): return lax.ppermute(value, 'dp', [(i, i ^ mask) for i in range(n_dp)])  35.4 us
  transfers between devices with their start and end apart: 82, of which 25 were waited for; matrix products, arithmetic and copies ran while one was open for 31% of the time, Pallas kernels for 2%

profile of v2, /device:TPU:1, one launch (start us, length us, event | category | flops | bytes accessed | tf_op | source)
XLA Modules:
  0.0 1086.6 jit_solution(11946016334768156191)
XLA Ops:
  48.1 22.0 %collective-permute-done.9.refs_2_ = bf16[176,4224]{1,0:T(8,128)(2,1)} collective-permute-done((bf16[176,4224]{1,0:T(8,128)(2,1)}, bf16[176,4224]{1,0:T(8,128)(2,1)}, u32[]{:S(2)}, u32[]{:S(2)}) %collective-permute-start.9) | collective-permute-done | bytes 1486880 | tf_op jit(solution)/shard_map/ppermute | solution.py:290
  99.4 8.5 assemble.7
  108.0 6.8 fusion.196
  121.1 5.7 all-to-all-start
  134.1 58.8 %all-to-all-done.refs_0_ = bf16[8,2,3,88,256]{4,3,2,1,0:T(8,128)(2,1)} async-done(((bf16[8,2,3,88,256]{4,3,2,1,0:T(8,128)(2,1)}), bf16[8,2,3,88,256]{4,3,2,1,0:T(8,128)(2,1)}, u32[]{:S(2)}, u32[]{:S(2)}) %all-to-all-start) | async-done | bytes 2162720 | tf_op jit(solution)/shard_map/all_to_all | solution.py:566
  205.4 13.3 %attend_forward.1 = (bf16[8,2,1,88,256]{4,3,2,1,0:T(8,128)(2,1)}, f32[2,2,1,1024]{3,2,1,0:T(1,128)S(1)}) custom-call(bf16[8,2,3,88,256]{4,3,2,1,0:T(8,128)(2,1)} %all-to-all-done.refs_0_, f32[8,128]{1,0:T(8,128)S(1)} %add.1090.refs_1_), custom_call_target="tpu_custom_call" | custom-call | flops 1024 | bytes 1024 | tf_op jit(solution)/shard_map/attend_forward/pallas_call | solution.py:243
  232.4 17.6 %collective-permute-done.20 = bf16[352,1536]{1,0:T(8,128)(2,1)} collective-permute-done((bf16[352,1536]{1,0:T(8,128)(2,1)}, bf16[352,1536]{1,0:T(8,128)(2,1)}, u32[]{:S(2)}, u32[]{:S(2)}) %collective-permute-start.20) | collective-permute-done | bytes 1081376 | tf_op jit(solution)/shard_map/ppermute | solution.py:290
  299.5 13.8 %collective-permute-done.23 = bf16[256,1408]{1,0:T(8,128)(2,1)S(1)} collective-permute-done((bf16[256,1408]{1,0:T(8,128)(2,1)S(1)}, bf16[256,1408]{1,0:T(8,128)(2,1)S(1)}, u32[]{:S(2)}, u32[]{:S(2)}) %collective-permute-start.23) | collective-permute-done | bytes 720928 | tf_op jit(solution)/shard_map/ppermute | solution.py:290
  322.6 6.2 collective-permute-done.27
  333.6 9.9 multiply_convert_fusion
  343.5 12.8 %fusion.8 = bf16[1536,1024]{1,0:T(8,128)(2,1)S(1)} fusion(f32[1536,1024]{1,0:T(8,128)} %get-tuple-element.233, bf16[1536,1408]{1,0:T(8,128)(2,1)S(1)} %bitcast.460, bf16[512,1408]{1,0:T(8,128)(2,1)S(1)} %collective-permute-done.28, bf16[256,1408]{1,0:T(8,128)(2,1)S(1)} %add_convert_fusion.45, bf16[256,1408]{1,0:T(8,128)(2,1)} %bitcast.54), kind=kOutput, calls=%fused_computation.15 | convolution fusion | flops 4469293056 | bytes 16646144 | tf_op jit(solution)/shard_map/dot_general | solution.py:21
  378.8 5.7 fusion.197
  400.3 10.4 collective-permute-done.30
  411.4 14.6 %collective-permute-done.26 = bf16[256,1408]{1,0:T(8,128)(2,1)S(1)} collective-permute-done((bf16[256,1408]{1,0:T(8,128)(2,1)S(1)}, bf16[256,1408]{1,0:T(8,128)(2,1)S(1)}, u32[]{:S(2)}, u32[]{:S(2)}) %collective-permute-start.26) | collective-permute-done | bytes 720928 | tf_op jit(solution)/shard_map/ppermute | solution.py:290
  499.4 6.0 add_convert_fusion.19
  511.0 17.9 %attend_backward.1 = bf16[8,2,3,88,256]{4,3,2,1,0:T(8,128)(2,1)} custom-call(bf16[8,2,3,88,256]{4,3,2,1,0:T(8,128)(2,1)} %all-to-all-done.refs_0_, f32[2,2,1,1024]{3,2,1,0:T(1,128)S(1)} %get-tuple-element.26.refs_1_, bf16[8,2,1,88,256]{4,3,2,1,0:T(8,128)(2,1)S(1)} %all-to-all-done.2.refs_2_, f32[8,128]{1,0:T(8,128)S(1)} %add.1154.refs_3_), custom_call_target="tpu_custom_call" | custom-call | flops 1024 | bytes 1024 | tf_op jit(solution)/shard_map/attend_backward/pallas_call | solution.py:243
  528.9 5.2 all-to-all-start.3
  542.1 49.8 %collective-permute-done.36 = bf16[2,3,176,1408]{3,2,1,0:T(8,128)(2,1)} collective-permute-done((bf16[2,3,176,1408]{3,2,1,0:T(8,128)(2,1)}, bf16[2,3,176,1408]{3,2,1,0:T(8,128)(2,1)}, u32[]{:S(2)}, u32[]{:S(2)}) %collective-permute-start.36) | collective-permute-done | bytes 2973728 | tf_op jit(solution)/shard_map/ppermute | solution.py:311
  605.1 7.8 convolution_convert_fusion
  612.8 5.7 constant_dynamic-slice_fusion.14
  644.7 5.1 add_convert_fusion.15
  652.8 9.6 multiply_reduce_fusion.7
  665.5 58.5 %collective-permute-done.43 = bf16[384,1408]{1,0:T(8,128)(2,1)} collective-permute-done((bf16[384,1408]{1,0:T(8,128)(2,1)}, bf16[384,1408]{1,0:T(8,128)(2,1)}, u32[]{:S(2)}, u32[]{:S(2)}) %collective-permute-start.43) | collective-permute-done | bytes 1081376 | tf_op jit(solution)/shard_map/ppermute | solution.py:296
  749.9 6.3 multiply_reduce_fusion.2
  765.3 18.1 %collective-permute-done.41 = bf16[2,1,176,4224]{3,2,1,0:T(8,128)(2,1)S(1)} collective-permute-done((bf16[2,1,176,4224]{3,2,1,0:T(8,128)(2,1)S(1)}, bf16[2,1,176,4224]{3,2,1,0:T(8,128)(2,1)S(1)}, u32[]{:S(2)}, u32[]{:S(2)}) %collective-permute-start.41) | collective-permute-done | bytes 2973728 | tf_op jit(solution)/shard_map/ppermute | solution.py:311
  830.1 18.9 %collective-permute-done.45 = bf16[3,88,1408]{2,1,0:T(8,128)(2,1)S(1)} collective-permute-done((bf16[3,88,1408]{2,1,0:T(8,128)(2,1)}, bf16[3,88,1408]{2,1,0:T(8,128)(2,1)S(1)}, u32[]{:S(2)}, u32[]{:S(2)}) %collective-permute-start.45) | collective-permute-done | bytes 743456 | tf_op jit(solution)/shard_map/ppermute | solution.py:296
  890.2 11.5 %collective-permute-done.52 = f32[18656]{0:T(1024)} collective-permute-done((f32[18656]{0:T(1024)S(1)}, f32[18656]{0:T(1024)}, u32[]{:S(2)}, u32[]{:S(2)}) %collective-permute-start.52) | collective-permute-done | bytes 74656 | tf_op jit(solution)/shard_map/ppermute | solution.py:293
  919.6 54.5 %collective-permute-done.62 = bf16[1,88,4224]{2,1,0:T(8,128)(2,1)S(1)} collective-permute-done((bf16[1,88,4224]{2,1,0:T(8,128)(2,1)}, bf16[1,88,4224]{2,1,0:T(8,128)(2,1)S(1)}, u32[]{:S(2)}, u32[]{:S(2)}) %collective-permute-start.62) | collective-permute-done | bytes 743456 | tf_op jit(solution)/shard_map/ppermute | solution.py:296
  982.9 6.7 maximum_convert_fusion
  991.5 7.8 collective-permute-done.60
  1018.3 15.9 %collective-permute-done.65 = bf16[2,3,88,1408]{3,2,1,0:T(8,128)(2,1)S(1)} collective-permute-done((bf16[2,3,88,1408]{3,2,1,0:T(8,128)(2,1)S(1)}, bf16[2,3,88,1408]{3,2,1,0:T(8,128)(2,1)S(1)}, u32[]{:S(2)}, u32[]{:S(2)}) %collective-permute-start.65) | collective-permute-done | bytes 1486880 | tf_op jit(solution)/shard_map/ppermute | solution.py:311
  1052.4 8.1 copy.173
  (751 shorter events, 487.7 us)
Async XLA Ops:
  7.2 68.2 %all-gather.3.cloned.1.call-start = ((), (), s32[]{:S(2)}) async-start(), calls=%async_computation.6 | async-start | bytes 1548288 | tf_op jit(solution)/shard_map/all_gather | solution.py:528
  7.3 40.5 %collective-permute-start.6 = (bf16[256,352]{0,1:T(8,128)(2,1)}, bf16[256,352]{0,1:T(8,128)(2,1)}, u32[]{:S(2)}, u32[]{:S(2)}) collective-permute-start(bf16[256,352]{0,1:T(8,128)(2,1)} %bitcast.446), channel_id=1, source_target_pairs={{0,8},{8,0},{16,24},{24,16},{1,9},{9,1},{17,25},{25,17},{2,10},{10... | collective-permute-start | bytes 540680 | tf_op jit(solution)/shard_map/ppermute | solution.py:290
  18.9 51.2 %collective-permute-start.9 = (bf16[176,4224]{1,0:T(8,128)(2,1)}, bf16[176,4224]{1,0:T(8,128)(2,1)}, u32[]{:S(2)}, u32[]{:S(2)}) collective-permute-start(bf16[176,4224]{1,0:T(8,128)(2,1)} %dynamic-slice_bitcast_fusion.4), channel_id=1, source_target_pairs={{0,16},{8,24},{16,0},{24,8},{1,17},{9,25},{17,1},{25,9},{2,18},{10... | collective-permute-start | bytes 4460552 | tf_op jit(solution)/shard_map/ppermute | solution.py:290
  47.7 51.6 %collective-permute-start.8 = (bf16[352,4224]{1,0:T(8,128)(2,1)}, bf16[352,4224]{1,0:T(8,128)(2,1)}, u32[]{:S(2)}, u32[]{:S(2)}) collective-permute-start(bf16[352,4224]{1,0:T(8,128)(2,1)} %refs_0_.3), channel_id=1, source_target_pairs={{0,8},{8,0},{16,24},{24,16},{1,9},{9,1},{17,25},{25,17},{2,10},{10... | collective-permute-start | bytes 8921096 | tf_op jit(solution)/shard_map/ppermute | solution.py:290
  121.1 71.9 %all-to-all-start = ((bf16[8,2,3,88,256]{4,3,2,1,0:T(8,128)(2,1)}), bf16[8,2,3,88,256]{4,3,2,1,0:T(8,128)(2,1)}, u32[]{:S(2)}, u32[]{:S(2)}) async-start(bf16[8,2,3,88,256]{4,3,2,1,0:T(8,128)(2,1)} %qkv_norm.1), calls=%async_computation | async-start | bytes 4325376 | tf_op jit(solution)/shard_map/all_to_all | solution.py:566
  126.8 127.4 %all-gather.5.cloned.1.call-start = ((), (), s32[]{:S(2)}) async-start(), calls=%async_computation.7 | async-start | bytes 4866048 | tf_op jit(solution)/shard_map/all_gather | solution.py:536
  129.4 66.0 %collective-permute-start.17 = (bf16[1056,1408]{1,0:T(8,128)(2,1)S(1)}, bf16[1056,1408]{1,0:T(8,128)(2,1)}, u32[]{:S(2)}, u32[]{:S(2)}) collective-permute-start(bf16[1056,1408]{1,0:T(8,128)(2,1)S(1)} %add_convert_fusion.1.refs_0_), channel_id=1, source_target_pairs={{0,16},{8,24},{16,0},{24,8},{1,17},{9,25},{17,1},{25,9},{2,18},{10... | collective-permute-start | bytes 8921096 | tf_op jit(solution)/shard_map/ppermute | solution.py:290
  132.7 126.4 %collective-permute-start.18 = (bf16[1056,1408]{1,0:T(8,128)(2,1)S(1)}, bf16[1056,1408]{1,0:T(8,128)(2,1)}, u32[]{:S(2)}, u32[]{:S(2)}) collective-permute-start(bf16[1056,1408]{1,0:T(8,128)(2,1)S(1)} %add_convert_fusion.1.refs_0_), channel_id=1, source_target_pairs={{0,8},{8,0},{16,24},{24,16},{1,9},{9,1},{17,25},{25,17},{2,10},{10... | collective-permute-start | bytes 8921096 | tf_op jit(solution)/shard_map/ppermute | solution.py:290
  199.5 59.6 %collective-permute-start.19 = (bf16[1056,1408]{1,0:T(8,128)(2,1)}, bf16[1056,1408]{1,0:T(8,128)(2,1)}, u32[]{:S(2)}, u32[]{:S(2)}) collective-permute-start(bf16[1056,1408]{1,0:T(8,128)(2,1)} %add_convert_fusion.refs_2_), channel_id=1, source_target_pairs={{0,8},{8,0},{16,24},{24,16},{1,9},{9,1},{17,25},{25,17},{2,10},{10... | collective-permute-start | bytes 8921096 | tf_op jit(solution)/shard_map/ppermute | solution.py:290
  202.5 47.5 %collective-permute-start.20 = (bf16[352,1536]{1,0:T(8,128)(2,1)}, bf16[352,1536]{1,0:T(8,128)(2,1)}, u32[]{:S(2)}, u32[]{:S(2)}) collective-permute-start(bf16[352,1536]{1,0:T(8,128)(2,1)} %get-tuple-element.145), channel_id=1, source_target_pairs={{0,16},{8,24},{16,0},{24,8},{1,17},{9,25},{17,1},{25,9},{2,18},{10... | collective-permute-start | bytes 3244040 | tf_op jit(solution)/shard_map/ppermute | solution.py:290
  219.9 43.8 %all-to-all-start.1 = ((bf16[8,2,1,88,256]{4,3,2,1,0:T(8,128)(2,1)}), bf16[8,2,1,88,256]{4,3,2,1,0:T(8,128)(2,1)}, u32[]{:S(2)}, u32[]{:S(2)}) async-start(bf16[8,2,1,88,256]{4,3,2,1,0:T(8,128)(2,1)} %get-tuple-element.25), calls=%async_computation.1 | async-start | bytes 1441792 | tf_op jit(solution)/shard_map/all_to_all | solution.py:566
  374.4 57.9 %collective-permute-start.33 = (bf16[768,1408]{1,0:T(8,128)(2,1)}, bf16[768,1408]{1,0:T(8,128)(2,1)S(1)}, u32[]{:S(2)}, u32[]{:S(2)}) collective-permute-start(bf16[768,1408]{1,0:T(8,128)(2,1)} %convolution_convert_fusion.8), channel_id=1, source_target_pairs={{0,1},{1,0},{2,3},{3,2},{4,5},{5,4},{6,7},{7,6},{8,10},{9,11},{10,... | collective-permute-start | bytes 6488072 | tf_op jit(solution)/shard_map/ppermute | solution.py:311
  397.8 52.9 %collective-permute-start.32 = (bf16[384,1408]{1,0:T(8,128)(2,1)}, bf16[384,1408]{1,0:T(8,128)(2,1)}, u32[]{:S(2)}, u32[]{:S(2)}) collective-permute-start(bf16[384,1408]{1,0:T(8,128)(2,1)} %add_convert_fusion.29), channel_id=1, source_target_pairs={{0,2},{1,3},{2,0},{3,1},{4,6},{5,7},{6,4},{7,5},{8,9},{9,8},{10,11... | collective-permute-start | bytes 3244040 | tf_op jit(solution)/shard_map/ppermute | solution.py:311
  528.9 69.7 %all-to-all-start.3 = ((bf16[8,2,3,88,256]{4,3,2,1,0:T(8,128)(2,1)}), bf16[8,2,3,88,256]{4,3,2,1,0:T(8,128)(2,1)S(1)}, u32[]{:S(2)}, u32[]{:S(2)}) async-start(bf16[8,2,3,88,256]{4,3,2,1,0:T(8,128)(2,1)} %attend_backward.1), calls=%async_computation.3 | async-start | bytes 4325376 | tf_op jit(solution)/shard_map/all_to_all | solution.py:566
  534.2 324.1 %reduce-scatter.3.cloned.1.call-start = ((), (), s32[]{:S(2)}) async-start(), calls=%async_computation.8 | async-start | bytes 2703360 | tf_op jit(solution)/shard_map/reduce_scatter | solution.py:732
  538.0 53.9 %collective-permute-start.36 = (bf16[2,3,176,1408]{3,2,1,0:T(8,128)(2,1)}, bf16[2,3,176,1408]{3,2,1,0:T(8,128)(2,1)}, u32[]{:S(2)}, u32[]{:S(2)}) collective-permute-start(bf16[2,3,176,1408]{3,2,1,0:T(8,128)(2,1)} %pad_maximum_fusion.5), channel_id=1, source_target_pairs={{0,16},{1,17},{2,18},{3,19},{4,20},{5,21},{6,22},{7,23},{8,9},{9,8... | collective-permute-start | bytes 8921096 | tf_op jit(solution)/shard_map/ppermute | solution.py:311
  628.7 113.2 %collective-permute-start.40 = (bf16[4,2,2,176,333]{4,3,1,2,0:T(8,128)(2,1)}, bf16[4,2,2,176,333]{4,3,1,2,0:T(8,128)(2,1)}, u32[]{:S(2)}, u32[]{:S(2)}) collective-permute-start(bf16[4,2,2,176,333]{4,3,1,2,0:T(8,128)(2,1)} %bitcast.403), channel_id=1, source_target_pairs={{0,1},{1,0},{2,3},{3,2},{4,5},{5,4},{6,7},{7,6},{8,9},{9,8},{10,11... | collective-permute-start | bytes 5626376 | tf_op jit(solution)/shard_map/ppermute | solution.py:293
  628.7 167.4 %collective-permute-start.47 = (bf16[384,1408]{1,0:T(8,128)(2,1)}, bf16[384,1408]{1,0:T(8,128)(2,1)}, u32[]{:S(2)}, u32[]{:S(2)}) collective-permute-start(bf16[384,1408]{1,0:T(8,128)(2,1)} %add_convert_fusion.27), channel_id=1, source_target_pairs={{0,4},{2,6},{4,0},{6,2},{1,5},{3,7},{5,1},{7,3},{8,12},{10,14},{12... | collective-permute-start | bytes 3244040 | tf_op jit(solution)/shard_map/ppermute | solution.py:296
  631.1 92.9 %collective-permute-start.43 = (bf16[384,1408]{1,0:T(8,128)(2,1)}, bf16[384,1408]{1,0:T(8,128)(2,1)}, u32[]{:S(2)}, u32[]{:S(2)}) collective-permute-start(bf16[384,1408]{1,0:T(8,128)(2,1)} %add_convert_fusion.24), channel_id=1, source_target_pairs={{0,4},{2,6},{4,0},{6,2},{1,5},{3,7},{5,1},{7,3},{8,12},{10,14},{12... | collective-permute-start | bytes 3244040 | tf_op jit(solution)/shard_map/ppermute | solution.py:296
  643.5 94.8 %collective-permute-start.39 = (bf16[3,88,1408]{2,1,0:T(8,128)(2,1)}, bf16[3,88,1408]{2,1,0:T(8,128)(2,1)S(1)}, u32[]{:S(2)}, u32[]{:S(2)}) collective-permute-start(bf16[3,88,1408]{2,1,0:T(8,128)(2,1)} %constant_dynamic-slice_fusion.15), channel_id=1, source_target_pairs={{0,2},{2,0},{4,6},{6,4},{1,3},{3,1},{5,7},{7,5},{8,10},{10,8},{12,... | collective-permute-start | bytes 2230280 | tf_op jit(solution)/shard_map/ppermute | solution.py:296
  728.0 62.9 %collective-permute-start.48 = (bf16[384,1408]{1,0:T(8,128)(2,1)}, bf16[384,1408]{1,0:T(8,128)(2,1)}, u32[]{:S(2)}, u32[]{:S(2)}) collective-permute-start(bf16[384,1408]{1,0:T(8,128)(2,1)} %add_convert_fusion.23), channel_id=1, source_target_pairs={{0,2},{1,3},{2,0},{3,1},{4,6},{5,7},{6,4},{7,5},{8,9},{9,8},{10,11... | collective-permute-start | bytes 3244040 | tf_op jit(solution)/shard_map/ppermute | solution.py:311
  745.5 305.1 %reduce-scatter.5.cloned.1.call-start = ((), (), s32[]{:S(2)}) async-start(), calls=%async_computation.9 | async-start | bytes 860160 | tf_op jit(solution)/shard_map/reduce_scatter | solution.py:787
  765.0 59.4 %collective-permute-start.46 = (bf16[2,2,176,1408]{3,2,1,0:T(8,128)(2,1)}, bf16[2,2,176,1408]{3,2,1,0:T(8,128)(2,1)}, u32[]{:S(2)}, u32[]{:S(2)}) collective-permute-start(bf16[2,2,176,1408]{3,2,1,0:T(8,128)(2,1)} %pad_maximum_fusion.9), channel_id=1, source_target_pairs={{0,16},{1,17},{2,18},{3,19},{4,20},{5,21},{6,22},{7,23},{8,9},{9,8... | collective-permute-start | bytes 5947400 | tf_op jit(solution)/shard_map/ppermute | solution.py:311
  806.6 44.6 %collective-permute-start.44 = (bf16[1,176,4224]{2,1,0:T(8,128)(2,1)}, bf16[1,176,4224]{2,1,0:T(8,128)(2,1)S(1)}, u32[]{:S(2)}, u32[]{:S(2)}) collective-permute-start(bf16[1,176,4224]{2,1,0:T(8,128)(2,1)} %fusion.62), channel_id=1, source_target_pairs={{0,1},{1,0},{2,3},{3,2},{4,5},{5,4},{6,7},{7,6},{8,24},{9,25},{10,... | collective-permute-start | bytes 4460552 | tf_op jit(solution)/shard_map/ppermute | solution.py:311
  819.0 158.3 %collective-permute-start.61 = (bf16[2,384,1408]{2,1,0:T(8,128)(2,1)}, bf16[2,384,1408]{2,1,0:T(8,128)(2,1)}, u32[]{:S(2)}, u32[]{:S(2)}) collective-permute-start(bf16[2,384,1408]{2,1,0:T(8,128)(2,1)} %copy-done.49), channel_id=1, source_target_pairs={{0,1},{1,0},{2,3},{3,2},{4,5},{5,4},{6,7},{7,6},{8,10},{9,11},{10,... | collective-permute-start | bytes 6488072 | tf_op jit(solution)/shard_map/ppermute | solution.py:311
  823.0 58.9 %collective-permute-start.59 = (bf16[4,352,384]{2,1,0:T(8,128)(2,1)}, bf16[4,352,384]{2,1,0:T(8,128)(2,1)}, u32[]{:S(2)}, u32[]{:S(2)}) collective-permute-start(bf16[4,352,384]{2,1,0:T(8,128)(2,1)} %get-tuple-element.189), channel_id=1, source_target_pairs={{0,2},{1,3},{2,0},{3,1},{4,6},{5,7},{6,4},{7,5},{8,9},{9,8},{10,11... | collective-permute-start | bytes 3244040 | tf_op jit(solution)/shard_map/ppermute | solution.py:311
  861.2 48.7 %collective-permute-start.55 = (bf16[2,176,1408]{2,1,0:T(8,128)(2,1)}, bf16[2,176,1408]{2,1,0:T(8,128)(2,1)}, u32[]{:S(2)}, u32[]{:S(2)}) collective-permute-start(bf16[2,176,1408]{2,1,0:T(8,128)(2,1)} %fusion.118), channel_id=1, source_target_pairs={{0,1},{1,0},{2,3},{3,2},{4,5},{5,4},{6,7},{7,6},{8,24},{9,25},{10,... | collective-permute-start | bytes 2973704 | tf_op jit(solution)/shard_map/ppermute | solution.py:311
  906.3 97.2 %collective-permute-start.67 = (bf16[2,4,352,384]{3,2,1,0:T(8,128)(2,1)}, bf16[2,4,352,384]{3,2,1,0:T(8,128)(2,1)}, u32[]{:S(2)}, u32[]{:S(2)}) collective-permute-start(bf16[2,4,352,384]{3,2,1,0:T(8,128)(2,1)} %add_convert_fusion.4), channel_id=1, source_target_pairs={{0,1},{1,0},{2,3},{3,2},{4,5},{5,4},{6,7},{7,6},{8,10},{9,11},{10,... | collective-permute-start | bytes 6488072 | tf_op jit(solution)/shard_map/ppermute | solution.py:311
  907.3 135.2 %collective-permute-start.72 = (bf16[2,256,352]{1,2,0:T(8,128)(2,1)}, bf16[2,256,352]{1,2,0:T(8,128)(2,1)}, u32[]{:S(2)}, u32[]{:S(2)}) collective-permute-start(bf16[2,256,352]{1,2,0:T(8,128)(2,1)} %bitcast.405), channel_id=1, source_target_pairs={{0,8},{8,0},{16,24},{24,16},{1,9},{9,1},{17,25},{25,17},{2,10},{10... | collective-permute-start | bytes 1081352 | tf_op jit(solution)/shard_map/ppermute | solution.py:290
  909.9 64.2 %collective-permute-start.62 = (bf16[1,88,4224]{2,1,0:T(8,128)(2,1)}, bf16[1,88,4224]{2,1,0:T(8,128)(2,1)S(1)}, u32[]{:S(2)}, u32[]{:S(2)}) collective-permute-start(bf16[1,88,4224]{2,1,0:T(8,128)(2,1)} %constant_dynamic-slice_fusion.12), channel_id=1, source_target_pairs={{0,2},{2,0},{4,6},{6,4},{1,3},{3,1},{5,7},{7,5},{8,10},{10,8},{12,... | collective-permute-start | bytes 2230280 | tf_op jit(solution)/shard_map/ppermute | solution.py:296
  914.3 130.1 %collective-permute-start.54 = (f32[18656]{0:T(1024)S(1)}, f32[18656]{0:T(1024)S(1)}, u32[]{:S(2)}, u32[]{:S(2)}) collective-permute-start(f32[18656]{0:T(1024)S(1)} %add.1238), channel_id=1, source_target_pairs={{0,4},{2,6},{4,0},{6,2},{1,5},{3,7},{5,1},{7,3},{8,12},{10,14},{12... | collective-permute-start | bytes 223880 | tf_op jit(solution)/shard_map/ppermute | solution.py:296
  974.8 40.1 %collective-permute-start.66 = (bf16[1,88,4224]{2,1,0:T(8,128)(2,1)S(1)}, bf16[1,88,4224]{2,1,0:T(8,128)(2,1)S(1)}, u32[]{:S(2)}, u32[]{:S(2)}) collective-permute-start(bf16[1,88,4224]{2,1,0:T(8,128)(2,1)S(1)} %add_convert_fusion.41), channel_id=1, source_target_pairs={{0,4},{2,6},{4,0},{6,2},{1,5},{3,7},{5,1},{7,3},{8,12},{10,14},{12... | collective-permute-start | bytes 2230280 | tf_op jit(solution)/shard_map/ppermute | solution.py:296
  (201 other events, 2454.2 us)
Sparse Core Ops, SparseCore 0:
  12.6 45.2 all-gather.2
  132.8 101.4 all-gather.4
  745.6 44.1 reduce-scatter.2
  910.0 31.5 reduce-scatter.4

commit v3 on v2

--- a/solution.py
+++ b/solution.py
@@ -422,7 +422,7 @@
             mask *= 2
         return value
 
-    def shard_sums(blocks):
+    def shard_sums(blocks, joined=False):
         number, (_, _, count, columns) = len(blocks), blocks[0].shape
 
         def side(which):
@@ -470,7 +470,7 @@
         pair = quarter_pair(own, token)
         token = yield pair
         full = quarters_in_order(pair, 1, token)
-        yield [full[i] for i in range(number)]
+        yield [full.reshape(-1, columns)] if joined else [full[i] for i in range(number)]
 
     def as_shards(grad):
         return grad.reshape((n_dp // 2, 2, -1) + grad.shape[1:])
@@ -725,7 +725,7 @@
     grad_one_bf = (grad_two + back_one).astype(BF)
     skip_blocks = dot(skip_bf, grad_one_bf, 0, 0).astype(BF)
     skip_blocks = skip_blocks.reshape(n_dp // 2, 2, 2, -1, width)
-    end = shard_sums([skip_blocks[:, :, i] for i in range(2)])
+    end = shard_sums([skip_blocks[:, :, i] for i in range(2)], joined=True)
     next(end)
     grad_skip_norm = dot(grad_one_bf, skip_full, 1, 1)
     grad_tkv = plus(tkv_keep, tkv_got, grad_one_bf)
@@ -768,8 +768,7 @@
     step(late)
     step(end)
     (qkv_grad,) = step(late)
-    skip_parts = step(end)
-    skip_grad_w = jnp.concatenate(skip_parts, axis=0)
+    (skip_grad_w,) = step(end)
     back_joined = back_joined.astype(BF).reshape(batch, length, 2 * width)
 
 

time: 1100 us -> 1100 us (level)
  no operation moved by 1% of the time
where the time goes in v3:
time: 1100 us; the launch traced here: 1090 us
  waiting for transfers between devices  408 us (37%)
  other arithmetic  166 us (15%)
  local copies, waits for them, and re-layouts  145 us (13%)
  matrix products  133 us (12%)
  starting transfers between devices  93.6 us (9%)
  between operations  79.1 us (7%)
  Pallas kernels  61.7 us (6%)
    ppermute x10, waiting for transfers between devices, zperm(): return lax.ppermute(value, 'z', [(i, i ^ mask) for i in range(n_seq // 2)])  140 us
    dot_general x24, matrix products, dot(): lax.dot_general(left, right, (((left_dim,), (right_dim,)), ((), ())), pre...  107 us
    ppermute x22, waiting for transfers between devices, mixed(): return lax.ppermute(value, ('dp', 'z', 'x'), pairs)  98.1 us
    ppermute x39, waiting for transfers between devices, dperm(): return lax.ppermute(value, 'dp', [(i, i ^ mask) for i in range(n_dp)])  95.5 us
    all_to_all x4, waiting for transfers between devices, exchange(): return lax.all_to_all(value, SEQ, split_axis=0, concat_axis=0, tiled=True)  62.6 us
    convert_element_type x25, other arithmetic, plus(): return total.astype(BF)  57.9 us
    slice x46, local copies, waits for them, and re-layouts, gate(): corner = value[(0,) * value.ndim].astype(F32)  37.4 us
    ppermute x39, starting transfers between devices, dperm(): return lax.ppermute(value, 'dp', [(i, i ^ mask) for i in range(n_dp)])  35.4 us
  transfers between devices with their start and end apart: 82, of which 25 were waited for; matrix products, arithmetic and copies ran while one was open for 31% of the time, Pallas kernels for 2%

profile of v3, /device:TPU:1, one launch (start us, length us, event | category | flops | bytes accessed | tf_op | source)
XLA Modules:
  0.0 1086.5 jit_solution(2319999938258670053)
XLA Ops:
  48.1 22.0 %collective-permute-done.9.refs_2_ = bf16[176,4224]{1,0:T(8,128)(2,1)} collective-permute-done((bf16[176,4224]{1,0:T(8,128)(2,1)}, bf16[176,4224]{1,0:T(8,128)(2,1)}, u32[]{:S(2)}, u32[]{:S(2)}) %collective-permute-start.9) | collective-permute-done | bytes 1486880 | tf_op jit(solution)/shard_map/ppermute | solution.py:290
  99.4 8.5 assemble.7
  108.0 6.8 fusion.196
  121.1 5.7 all-to-all-start
  134.1 58.8 %all-to-all-done.refs_0_ = bf16[8,2,3,88,256]{4,3,2,1,0:T(8,128)(2,1)} async-done(((bf16[8,2,3,88,256]{4,3,2,1,0:T(8,128)(2,1)}), bf16[8,2,3,88,256]{4,3,2,1,0:T(8,128)(2,1)}, u32[]{:S(2)}, u32[]{:S(2)}) %all-to-all-start) | async-done | bytes 2162720 | tf_op jit(solution)/shard_map/all_to_all | solution.py:566
  205.4 13.3 %attend_forward.1 = (bf16[8,2,1,88,256]{4,3,2,1,0:T(8,128)(2,1)}, f32[2,2,1,1024]{3,2,1,0:T(1,128)S(1)}) custom-call(bf16[8,2,3,88,256]{4,3,2,1,0:T(8,128)(2,1)} %all-to-all-done.refs_0_, f32[8,128]{1,0:T(8,128)S(1)} %add.1090.refs_1_), custom_call_target="tpu_custom_call" | custom-call | flops 1024 | bytes 1024 | tf_op jit(solution)/shard_map/attend_forward/pallas_call | solution.py:243
  232.4 17.6 %collective-permute-done.20 = bf16[352,1536]{1,0:T(8,128)(2,1)} collective-permute-done((bf16[352,1536]{1,0:T(8,128)(2,1)}, bf16[352,1536]{1,0:T(8,128)(2,1)}, u32[]{:S(2)}, u32[]{:S(2)}) %collective-permute-start.20) | collective-permute-done | bytes 1081376 | tf_op jit(solution)/shard_map/ppermute | solution.py:290
  299.5 13.8 %collective-permute-done.23 = bf16[256,1408]{1,0:T(8,128)(2,1)S(1)} collective-permute-done((bf16[256,1408]{1,0:T(8,128)(2,1)S(1)}, bf16[256,1408]{1,0:T(8,128)(2,1)S(1)}, u32[]{:S(2)}, u32[]{:S(2)}) %collective-permute-start.23) | collective-permute-done | bytes 720928 | tf_op jit(solution)/shard_map/ppermute | solution.py:290
  322.6 6.2 collective-permute-done.27
  333.7 9.9 multiply_convert_fusion
  343.6 12.8 %fusion.8 = bf16[1536,1024]{1,0:T(8,128)(2,1)S(1)} fusion(f32[1536,1024]{1,0:T(8,128)} %get-tuple-element.231, bf16[1536,1408]{1,0:T(8,128)(2,1)S(1)} %bitcast.459, bf16[512,1408]{1,0:T(8,128)(2,1)S(1)} %collective-permute-done.28, bf16[256,1408]{1,0:T(8,128)(2,1)S(1)} %add_convert_fusion.45, bf16[256,1408]{1,0:T(8,128)(2,1)} %bitcast.54), kind=kOutput, calls=%fused_computation.15 | convolution fusion | flops 4469293056 | bytes 16646144 | tf_op jit(solution)/shard_map/dot_general | solution.py:21
  378.8 5.7 fusion.197
  400.3 10.4 collective-permute-done.30
  411.5 14.6 %collective-permute-done.26 = bf16[256,1408]{1,0:T(8,128)(2,1)S(1)} collective-permute-done((bf16[256,1408]{1,0:T(8,128)(2,1)S(1)}, bf16[256,1408]{1,0:T(8,128)(2,1)S(1)}, u32[]{:S(2)}, u32[]{:S(2)}) %collective-permute-start.26) | collective-permute-done | bytes 720928 | tf_op jit(solution)/shard_map/ppermute | solution.py:290
  499.5 6.0 add_convert_fusion.19
  511.0 17.9 %attend_backward.1 = bf16[8,2,3,88,256]{4,3,2,1,0:T(8,128)(2,1)} custom-call(bf16[8,2,3,88,256]{4,3,2,1,0:T(8,128)(2,1)} %all-to-all-done.refs_0_, f32[2,2,1,1024]{3,2,1,0:T(1,128)S(1)} %get-tuple-element.26.refs_1_, bf16[8,2,1,88,256]{4,3,2,1,0:T(8,128)(2,1)S(1)} %all-to-all-done.2.refs_2_, f32[8,128]{1,0:T(8,128)S(1)} %add.1154.refs_3_), custom_call_target="tpu_custom_call" | custom-call | flops 1024 | bytes 1024 | tf_op jit(solution)/shard_map/attend_backward/pallas_call | solution.py:243
  529.0 5.2 all-to-all-start.3
  542.1 49.8 %collective-permute-done.36 = bf16[2,3,176,1408]{3,2,1,0:T(8,128)(2,1)} collective-permute-done((bf16[2,3,176,1408]{3,2,1,0:T(8,128)(2,1)}, bf16[2,3,176,1408]{3,2,1,0:T(8,128)(2,1)}, u32[]{:S(2)}, u32[]{:S(2)}) %collective-permute-start.36) | collective-permute-done | bytes 2973728 | tf_op jit(solution)/shard_map/ppermute | solution.py:311
  605.1 7.8 convolution_convert_fusion
  612.9 5.7 constant_dynamic-slice_fusion.14
  644.7 5.1 add_convert_fusion.15
  652.8 9.6 multiply_reduce_fusion.7
  665.5 58.5 %collective-permute-done.43 = bf16[384,1408]{1,0:T(8,128)(2,1)} collective-permute-done((bf16[384,1408]{1,0:T(8,128)(2,1)}, bf16[384,1408]{1,0:T(8,128)(2,1)}, u32[]{:S(2)}, u32[]{:S(2)}) %collective-permute-start.43) | collective-permute-done | bytes 1081376 | tf_op jit(solution)/shard_map/ppermute | solution.py:296
  750.0 6.3 multiply_reduce_fusion.2
  765.4 18.2 %collective-permute-done.41 = bf16[2,1,176,4224]{3,2,1,0:T(8,128)(2,1)S(1)} collective-permute-done((bf16[2,1,176,4224]{3,2,1,0:T(8,128)(2,1)S(1)}, bf16[2,1,176,4224]{3,2,1,0:T(8,128)(2,1)S(1)}, u32[]{:S(2)}, u32[]{:S(2)}) %collective-permute-start.41) | collective-permute-done | bytes 2973728 | tf_op jit(solution)/shard_map/ppermute | solution.py:311
  830.1 18.9 %collective-permute-done.45 = bf16[3,88,1408]{2,1,0:T(8,128)(2,1)S(1)} collective-permute-done((bf16[3,88,1408]{2,1,0:T(8,128)(2,1)}, bf16[3,88,1408]{2,1,0:T(8,128)(2,1)S(1)}, u32[]{:S(2)}, u32[]{:S(2)}) %collective-permute-start.45) | collective-permute-done | bytes 743456 | tf_op jit(solution)/shard_map/ppermute | solution.py:296
  890.2 11.5 %collective-permute-done.52 = f32[18656]{0:T(1024)} collective-permute-done((f32[18656]{0:T(1024)S(1)}, f32[18656]{0:T(1024)}, u32[]{:S(2)}, u32[]{:S(2)}) %collective-permute-start.52) | collective-permute-done | bytes 74656 | tf_op jit(solution)/shard_map/ppermute | solution.py:293
  919.7 54.3 %collective-permute-done.62 = bf16[1,88,4224]{2,1,0:T(8,128)(2,1)S(1)} collective-permute-done((bf16[1,88,4224]{2,1,0:T(8,128)(2,1)}, bf16[1,88,4224]{2,1,0:T(8,128)(2,1)S(1)}, u32[]{:S(2)}, u32[]{:S(2)}) %collective-permute-start.62) | collective-permute-done | bytes 743456 | tf_op jit(solution)/shard_map/ppermute | solution.py:296
  983.0 6.7 maximum_convert_fusion
  991.6 7.9 collective-permute-done.60
  1018.2 16.1 %collective-permute-done.65 = bf16[2,3,88,1408]{3,2,1,0:T(8,128)(2,1)S(1)} collective-permute-done((bf16[2,3,88,1408]{3,2,1,0:T(8,128)(2,1)S(1)}, bf16[2,3,88,1408]{3,2,1,0:T(8,128)(2,1)S(1)}, u32[]{:S(2)}, u32[]{:S(2)}) %collective-permute-start.65) | collective-permute-done | bytes 1486880 | tf_op jit(solution)/shard_map/ppermute | solution.py:311
  1052.5 8.1 copy.173
  (750 shorter events, 487.4 us)
Async XLA Ops:
  7.2 68.2 %all-gather.3.cloned.1.call-start = ((), (), s32[]{:S(2)}) async-start(), calls=%async_computation.6 | async-start | bytes 1548288 | tf_op jit(solution)/shard_map/all_gather | solution.py:528
  7.3 40.5 %collective-permute-start.6 = (bf16[256,352]{0,1:T(8,128)(2,1)}, bf16[256,352]{0,1:T(8,128)(2,1)}, u32[]{:S(2)}, u32[]{:S(2)}) collective-permute-start(bf16[256,352]{0,1:T(8,128)(2,1)} %bitcast.445), channel_id=1, source_target_pairs={{0,8},{8,0},{16,24},{24,16},{1,9},{9,1},{17,25},{25,17},{2,10},{10... | collective-permute-start | bytes 540680 | tf_op jit(solution)/shard_map/ppermute | solution.py:290
  18.9 51.2 %collective-permute-start.9 = (bf16[176,4224]{1,0:T(8,128)(2,1)}, bf16[176,4224]{1,0:T(8,128)(2,1)}, u32[]{:S(2)}, u32[]{:S(2)}) collective-permute-start(bf16[176,4224]{1,0:T(8,128)(2,1)} %dynamic-slice_bitcast_fusion.4), channel_id=1, source_target_pairs={{0,16},{8,24},{16,0},{24,8},{1,17},{9,25},{17,1},{25,9},{2,18},{10... | collective-permute-start | bytes 4460552 | tf_op jit(solution)/shard_map/ppermute | solution.py:290
  47.8 51.6 %collective-permute-start.8 = (bf16[352,4224]{1,0:T(8,128)(2,1)}, bf16[352,4224]{1,0:T(8,128)(2,1)}, u32[]{:S(2)}, u32[]{:S(2)}) collective-permute-start(bf16[352,4224]{1,0:T(8,128)(2,1)} %refs_0_.3), channel_id=1, source_target_pairs={{0,8},{8,0},{16,24},{24,16},{1,9},{9,1},{17,25},{25,17},{2,10},{10... | collective-permute-start | bytes 8921096 | tf_op jit(solution)/shard_map/ppermute | solution.py:290
  121.1 71.8 %all-to-all-start = ((bf16[8,2,3,88,256]{4,3,2,1,0:T(8,128)(2,1)}), bf16[8,2,3,88,256]{4,3,2,1,0:T(8,128)(2,1)}, u32[]{:S(2)}, u32[]{:S(2)}) async-start(bf16[8,2,3,88,256]{4,3,2,1,0:T(8,128)(2,1)} %qkv_norm.1), calls=%async_computation | async-start | bytes 4325376 | tf_op jit(solution)/shard_map/all_to_all | solution.py:566
  126.8 127.4 %all-gather.5.cloned.1.call-start = ((), (), s32[]{:S(2)}) async-start(), calls=%async_computation.7 | async-start | bytes 4866048 | tf_op jit(solution)/shard_map/all_gather | solution.py:536
  129.4 66.0 %collective-permute-start.17 = (bf16[1056,1408]{1,0:T(8,128)(2,1)S(1)}, bf16[1056,1408]{1,0:T(8,128)(2,1)}, u32[]{:S(2)}, u32[]{:S(2)}) collective-permute-start(bf16[1056,1408]{1,0:T(8,128)(2,1)S(1)} %add_convert_fusion.1.refs_0_), channel_id=1, source_target_pairs={{0,16},{8,24},{16,0},{24,8},{1,17},{9,25},{17,1},{25,9},{2,18},{10... | collective-permute-start | bytes 8921096 | tf_op jit(solution)/shard_map/ppermute | solution.py:290
  132.7 126.4 %collective-permute-start.18 = (bf16[1056,1408]{1,0:T(8,128)(2,1)S(1)}, bf16[1056,1408]{1,0:T(8,128)(2,1)}, u32[]{:S(2)}, u32[]{:S(2)}) collective-permute-start(bf16[1056,1408]{1,0:T(8,128)(2,1)S(1)} %add_convert_fusion.1.refs_0_), channel_id=1, source_target_pairs={{0,8},{8,0},{16,24},{24,16},{1,9},{9,1},{17,25},{25,17},{2,10},{10... | collective-permute-start | bytes 8921096 | tf_op jit(solution)/shard_map/ppermute | solution.py:290
  199.5 59.6 %collective-permute-start.19 = (bf16[1056,1408]{1,0:T(8,128)(2,1)}, bf16[1056,1408]{1,0:T(8,128)(2,1)}, u32[]{:S(2)}, u32[]{:S(2)}) collective-permute-start(bf16[1056,1408]{1,0:T(8,128)(2,1)} %add_convert_fusion.refs_2_), channel_id=1, source_target_pairs={{0,8},{8,0},{16,24},{24,16},{1,9},{9,1},{17,25},{25,17},{2,10},{10... | collective-permute-start | bytes 8921096 | tf_op jit(solution)/shard_map/ppermute | solution.py:290
  202.6 47.5 %collective-permute-start.20 = (bf16[352,1536]{1,0:T(8,128)(2,1)}, bf16[352,1536]{1,0:T(8,128)(2,1)}, u32[]{:S(2)}, u32[]{:S(2)}) collective-permute-start(bf16[352,1536]{1,0:T(8,128)(2,1)} %get-tuple-element.145), channel_id=1, source_target_pairs={{0,16},{8,24},{16,0},{24,8},{1,17},{9,25},{17,1},{25,9},{2,18},{10... | collective-permute-start | bytes 3244040 | tf_op jit(solution)/shard_map/ppermute | solution.py:290
  219.9 43.8 %all-to-all-start.1 = ((bf16[8,2,1,88,256]{4,3,2,1,0:T(8,128)(2,1)}), bf16[8,2,1,88,256]{4,3,2,1,0:T(8,128)(2,1)}, u32[]{:S(2)}, u32[]{:S(2)}) async-start(bf16[8,2,1,88,256]{4,3,2,1,0:T(8,128)(2,1)} %get-tuple-element.25), calls=%async_computation.1 | async-start | bytes 1441792 | tf_op jit(solution)/shard_map/all_to_all | solution.py:566
  374.4 57.9 %collective-permute-start.33 = (bf16[768,1408]{1,0:T(8,128)(2,1)}, bf16[768,1408]{1,0:T(8,128)(2,1)S(1)}, u32[]{:S(2)}, u32[]{:S(2)}) collective-permute-start(bf16[768,1408]{1,0:T(8,128)(2,1)} %convolution_convert_fusion.8), channel_id=1, source_target_pairs={{0,1},{1,0},{2,3},{3,2},{4,5},{5,4},{6,7},{7,6},{8,10},{9,11},{10,... | collective-permute-start | bytes 6488072 | tf_op jit(solution)/shard_map/ppermute | solution.py:311
  397.9 52.8 %collective-permute-start.32 = (bf16[384,1408]{1,0:T(8,128)(2,1)}, bf16[384,1408]{1,0:T(8,128)(2,1)}, u32[]{:S(2)}, u32[]{:S(2)}) collective-permute-start(bf16[384,1408]{1,0:T(8,128)(2,1)} %add_convert_fusion.29), channel_id=1, source_target_pairs={{0,2},{1,3},{2,0},{3,1},{4,6},{5,7},{6,4},{7,5},{8,9},{9,8},{10,11... | collective-permute-start | bytes 3244040 | tf_op jit(solution)/shard_map/ppermute | solution.py:311
  529.0 69.7 %all-to-all-start.3 = ((bf16[8,2,3,88,256]{4,3,2,1,0:T(8,128)(2,1)}), bf16[8,2,3,88,256]{4,3,2,1,0:T(8,128)(2,1)S(1)}, u32[]{:S(2)}, u32[]{:S(2)}) async-start(bf16[8,2,3,88,256]{4,3,2,1,0:T(8,128)(2,1)} %attend_backward.1), calls=%async_computation.3 | async-start | bytes 4325376 | tf_op jit(solution)/shard_map/all_to_all | solution.py:566
  534.2 324.1 %reduce-scatter.3.cloned.1.call-start = ((), (), s32[]{:S(2)}) async-start(), calls=%async_computation.8 | async-start | bytes 2703360 | tf_op jit(solution)/shard_map/reduce_scatter | solution.py:732
  538.0 53.9 %collective-permute-start.36 = (bf16[2,3,176,1408]{3,2,1,0:T(8,128)(2,1)}, bf16[2,3,176,1408]{3,2,1,0:T(8,128)(2,1)}, u32[]{:S(2)}, u32[]{:S(2)}) collective-permute-start(bf16[2,3,176,1408]{3,2,1,0:T(8,128)(2,1)} %pad_maximum_fusion.4), channel_id=1, source_target_pairs={{0,16},{1,17},{2,18},{3,19},{4,20},{5,21},{6,22},{7,23},{8,9},{9,8... | collective-permute-start | bytes 8921096 | tf_op jit(solution)/shard_map/ppermute | solution.py:311
  628.7 113.2 %collective-permute-start.40 = (bf16[4,2,2,176,333]{4,3,1,2,0:T(8,128)(2,1)}, bf16[4,2,2,176,333]{4,3,1,2,0:T(8,128)(2,1)}, u32[]{:S(2)}, u32[]{:S(2)}) collective-permute-start(bf16[4,2,2,176,333]{4,3,1,2,0:T(8,128)(2,1)} %bitcast.402), channel_id=1, source_target_pairs={{0,1},{1,0},{2,3},{3,2},{4,5},{5,4},{6,7},{7,6},{8,9},{9,8},{10,11... | collective-permute-start | bytes 5626376 | tf_op jit(solution)/shard_map/ppermute | solution.py:293
  628.7 167.4 %collective-permute-start.47 = (bf16[384,1408]{1,0:T(8,128)(2,1)}, bf16[384,1408]{1,0:T(8,128)(2,1)}, u32[]{:S(2)}, u32[]{:S(2)}) collective-permute-start(bf16[384,1408]{1,0:T(8,128)(2,1)} %add_convert_fusion.27), channel_id=1, source_target_pairs={{0,4},{2,6},{4,0},{6,2},{1,5},{3,7},{5,1},{7,3},{8,12},{10,14},{12... | collective-permute-start | bytes 3244040 | tf_op jit(solution)/shard_map/ppermute | solution.py:296
  631.1 92.9 %collective-permute-start.43 = (bf16[384,1408]{1,0:T(8,128)(2,1)}, bf16[384,1408]{1,0:T(8,128)(2,1)}, u32[]{:S(2)}, u32[]{:S(2)}) collective-permute-start(bf16[384,1408]{1,0:T(8,128)(2,1)} %add_convert_fusion.24), channel_id=1, source_target_pairs={{0,4},{2,6},{4,0},{6,2},{1,5},{3,7},{5,1},{7,3},{8,12},{10,14},{12... | collective-permute-start | bytes 3244040 | tf_op jit(solution)/shard_map/ppermute | solution.py:296
  643.5 94.9 %collective-permute-start.39 = (bf16[3,88,1408]{2,1,0:T(8,128)(2,1)}, bf16[3,88,1408]{2,1,0:T(8,128)(2,1)S(1)}, u32[]{:S(2)}, u32[]{:S(2)}) collective-permute-start(bf16[3,88,1408]{2,1,0:T(8,128)(2,1)} %constant_dynamic-slice_fusion.15), channel_id=1, source_target_pairs={{0,2},{2,0},{4,6},{6,4},{1,3},{3,1},{5,7},{7,5},{8,10},{10,8},{12,... | collective-permute-start | bytes 2230280 | tf_op jit(solution)/shard_map/ppermute | solution.py:296
  728.1 62.9 %collective-permute-start.48 = (bf16[384,1408]{1,0:T(8,128)(2,1)}, bf16[384,1408]{1,0:T(8,128)(2,1)}, u32[]{:S(2)}, u32[]{:S(2)}) collective-permute-start(bf16[384,1408]{1,0:T(8,128)(2,1)} %add_convert_fusion.23), channel_id=1, source_target_pairs={{0,2},{1,3},{2,0},{3,1},{4,6},{5,7},{6,4},{7,5},{8,9},{9,8},{10,11... | collective-permute-start | bytes 3244040 | tf_op jit(solution)/shard_map/ppermute | solution.py:311
  745.6 305.2 %reduce-scatter.5.cloned.1.call-start = ((), (), s32[]{:S(2)}) async-start(), calls=%async_computation.9 | async-start | bytes 860160 | tf_op jit(solution)/shard_map/reduce_scatter | solution.py:786
  765.0 59.4 %collective-permute-start.46 = (bf16[2,2,176,1408]{3,2,1,0:T(8,128)(2,1)}, bf16[2,2,176,1408]{3,2,1,0:T(8,128)(2,1)}, u32[]{:S(2)}, u32[]{:S(2)}) collective-permute-start(bf16[2,2,176,1408]{3,2,1,0:T(8,128)(2,1)} %pad_maximum_fusion.8), channel_id=1, source_target_pairs={{0,16},{1,17},{2,18},{3,19},{4,20},{5,21},{6,22},{7,23},{8,9},{9,8... | collective-permute-start | bytes 5947400 | tf_op jit(solution)/shard_map/ppermute | solution.py:311
  806.6 44.5 %collective-permute-start.44 = (bf16[1,176,4224]{2,1,0:T(8,128)(2,1)}, bf16[1,176,4224]{2,1,0:T(8,128)(2,1)S(1)}, u32[]{:S(2)}, u32[]{:S(2)}) collective-permute-start(bf16[1,176,4224]{2,1,0:T(8,128)(2,1)} %fusion.62), channel_id=1, source_target_pairs={{0,1},{1,0},{2,3},{3,2},{4,5},{5,4},{6,7},{7,6},{8,24},{9,25},{10,... | collective-permute-start | bytes 4460552 | tf_op jit(solution)/shard_map/ppermute | solution.py:311
  819.1 158.5 %collective-permute-start.61 = (bf16[2,384,1408]{2,1,0:T(8,128)(2,1)}, bf16[2,384,1408]{2,1,0:T(8,128)(2,1)}, u32[]{:S(2)}, u32[]{:S(2)}) collective-permute-start(bf16[2,384,1408]{2,1,0:T(8,128)(2,1)} %copy-done.49), channel_id=1, source_target_pairs={{0,1},{1,0},{2,3},{3,2},{4,5},{5,4},{6,7},{7,6},{8,10},{9,11},{10,... | collective-permute-start | bytes 6488072 | tf_op jit(solution)/shard_map/ppermute | solution.py:311
  823.0 58.9 %collective-permute-start.59 = (bf16[4,352,384]{2,1,0:T(8,128)(2,1)}, bf16[4,352,384]{2,1,0:T(8,128)(2,1)}, u32[]{:S(2)}, u32[]{:S(2)}) collective-permute-start(bf16[4,352,384]{2,1,0:T(8,128)(2,1)} %get-tuple-element.187), channel_id=1, source_target_pairs={{0,2},{1,3},{2,0},{3,1},{4,6},{5,7},{6,4},{7,5},{8,9},{9,8},{10,11... | collective-permute-start | bytes 3244040 | tf_op jit(solution)/shard_map/ppermute | solution.py:311
  861.2 48.7 %collective-permute-start.55 = (bf16[2,176,1408]{2,1,0:T(8,128)(2,1)}, bf16[2,176,1408]{2,1,0:T(8,128)(2,1)}, u32[]{:S(2)}, u32[]{:S(2)}) collective-permute-start(bf16[2,176,1408]{2,1,0:T(8,128)(2,1)} %fusion.118), channel_id=1, source_target_pairs={{0,1},{1,0},{2,3},{3,2},{4,5},{5,4},{6,7},{7,6},{8,24},{9,25},{10,... | collective-permute-start | bytes 2973704 | tf_op jit(solution)/shard_map/ppermute | solution.py:311
  906.3 97.4 %collective-permute-start.67 = (bf16[2,4,352,384]{3,2,1,0:T(8,128)(2,1)}, bf16[2,4,352,384]{3,2,1,0:T(8,128)(2,1)}, u32[]{:S(2)}, u32[]{:S(2)}) collective-permute-start(bf16[2,4,352,384]{3,2,1,0:T(8,128)(2,1)} %add_convert_fusion.4), channel_id=1, source_target_pairs={{0,1},{1,0},{2,3},{3,2},{4,5},{5,4},{6,7},{7,6},{8,10},{9,11},{10,... | collective-permute-start | bytes 6488072 | tf_op jit(solution)/shard_map/ppermute | solution.py:311
  907.3 135.3 %collective-permute-start.72 = (bf16[2,256,352]{1,2,0:T(8,128)(2,1)}, bf16[2,256,352]{1,2,0:T(8,128)(2,1)}, u32[]{:S(2)}, u32[]{:S(2)}) collective-permute-start(bf16[2,256,352]{1,2,0:T(8,128)(2,1)} %bitcast.404), channel_id=1, source_target_pairs={{0,8},{8,0},{16,24},{24,16},{1,9},{9,1},{17,25},{25,17},{2,10},{10... | collective-permute-start | bytes 1081352 | tf_op jit(solution)/shard_map/ppermute | solution.py:290
  909.9 64.2 %collective-permute-start.62 = (bf16[1,88,4224]{2,1,0:T(8,128)(2,1)}, bf16[1,88,4224]{2,1,0:T(8,128)(2,1)S(1)}, u32[]{:S(2)}, u32[]{:S(2)}) collective-permute-start(bf16[1,88,4224]{2,1,0:T(8,128)(2,1)} %constant_dynamic-slice_fusion.12), channel_id=1, source_target_pairs={{0,2},{2,0},{4,6},{6,4},{1,3},{3,1},{5,7},{7,5},{8,10},{10,8},{12,... | collective-permute-start | bytes 2230280 | tf_op jit(solution)/shard_map/ppermute | solution.py:296
  914.3 130.2 %collective-permute-start.54 = (f32[18656]{0:T(1024)S(1)}, f32[18656]{0:T(1024)S(1)}, u32[]{:S(2)}, u32[]{:S(2)}) collective-permute-start(f32[18656]{0:T(1024)S(1)} %add.1238), channel_id=1, source_target_pairs={{0,4},{2,6},{4,0},{6,2},{1,5},{3,7},{5,1},{7,3},{8,12},{10,14},{12... | collective-permute-start | bytes 223880 | tf_op jit(solution)/shard_map/ppermute | solution.py:296
  974.8 40.4 %collective-permute-start.66 = (bf16[1,88,4224]{2,1,0:T(8,128)(2,1)S(1)}, bf16[1,88,4224]{2,1,0:T(8,128)(2,1)S(1)}, u32[]{:S(2)}, u32[]{:S(2)}) collective-permute-start(bf16[1,88,4224]{2,1,0:T(8,128)(2,1)S(1)} %add_convert_fusion.41), channel_id=1, source_target_pairs={{0,4},{2,6},{4,0},{6,2},{1,5},{3,7},{5,1},{7,3},{8,12},{10,14},{12... | collective-permute-start | bytes 2230280 | tf_op jit(solution)/shard_map/ppermute | solution.py:296
  (201 other events, 2454.0 us)
Sparse Core Ops, SparseCore 0:
  12.6 45.2 all-gather.2
  132.8 101.4 all-gather.4
  745.7 44.1 reduce-scatter.2
  910.0 31.7 reduce-scatter.4
